TPU v7x, 128 devices: a whole 4x4x4 slice. The times are simulated.
128 devices in a mesh: section: 4 (over z_hi, core), win: 32 (over z_lo, y, x).
Axes of the slice: x: 4, y: 4, z: 4 (z_hi: 2, z_lo: 2; z = z_hi * 2 + z_lo), core: 2. Of those that a mesh axis runs over, the one named last changes fastest.
Arguments:
- latent: bfloat16 [24, 256, 256], P(None, 'win'), may hold values from -6 to 6
- anchors: int32 [64, 2], P('win'), may hold values from 0 to 248, as said below
- in_proj: bfloat16 [256, 1280], replicated, may hold values from -0.375 to 0.375
- pos_embed: bfloat16 [256, 1280], replicated, may hold values from -6 to 6
- section_w1: bfloat16 [4, 1280, 2560], P('section'), may hold values from -0.15625 to 0.15625
- section_w2: bfloat16 [4, 2560, 1280], P('section'), may hold values from -0.125 to 0.125
- section_gain: float32 [4, 1280], P('section'), may hold values from 0.5 to 1.5
- skip_w: bfloat16 [2560, 1280], replicated, may hold values from -0.125 to 0.125
- out_proj: bfloat16 [1280, 256], replicated, may hold values from -0.15625 to 0.15625
Outputs:
- noise_avg: bfloat16 [24, 256, 256], P('section', 'win')
Inputs may be any that keep to these rules, and one draw needn't show every extreme that they name: Column 0 holds the row anchor, column 1 the column anchor; the windows are listed in an order drawn at random. Every column anchor that is a multiple of 8 below 256 appears in exactly 2 windows. Let g be a column anchor divided by 8. For even g, the row anchors of those windows are 0 and 8. For odd g, each row anchor lies anywhere from 0 to 8. Every token is covered by at least one window.
All inputs are finite; a program needn't handle non-finite values.
Results may differ from a plain program's by a relative error of at most 0.014.
Values may be sent and summed in bfloat16 or wider, within the bound.
No kernel may reach another device: no remote copies, remote signals or barrier semaphores. Data moves between devices by JAX's collectives and lax.ppermute only.
A program may use at most 128 MiB of HBM per device.

v0:
```python
import functools

import jax
import jax.numpy as jnp
from jax import lax
from jax.experimental import pallas as pl
from jax.experimental.pallas import tpu as pltpu
from jax.sharding import PartitionSpec as P

TILE = 16
STRIDE = 8
HALF = TILE // 2
ROUNDS = ((16, 2), (1, 4), (4, 4))
MIB = 1 << 20
COST = 16
F32 = jnp.float32
BF16 = jnp.bfloat16


def gelu(v):
    return jax.nn.gelu(v, approximate=True)


def normalise(v, gain):
    factor = lax.rsqrt(jnp.mean(v * v, axis=-1, keepdims=True) + 1e-06)
    return (v * factor * gain).astype(BF16)


def embed_rows(lat, inp, pos, anchors, half):
    width = lat.shape[-1]
    tiles = [
        lat[pl.ds(a, TILE)].astype(F32).reshape(TILE * HALF, width).astype(BF16) for a in anchors
    ]
    place = pos[:, half].astype(F32).reshape(TILE * HALF, pos.shape[-1])
    return [jnp.dot(t, inp[...], preferred_element_type=F32) + place for t in tiles]


def load_kernel(
    chunks, lat_h, inp_h, pos_h, gain_h, w1_h, w2_h,
    y, lat, inp, pos, gain_ref, w1, w2, norm, acc, sems,
):
    section, half = lax.axis_index("section"), lax.rem(lax.axis_index("win"), 2)
    hidden = w1.shape[1]
    size = hidden // chunks
    small = [(lat_h, lat), (inp_h, inp), (pos_h, pos), (gain_h, gain_ref)]
    copies = [pltpu.make_async_copy(a, b, sems.at[k]) for k, (a, b) in enumerate(small)]
    base = len(small)
    for c in range(chunks):
        cut = pl.ds(c * size, size)
        copies.append(pltpu.make_async_copy(w1_h.at[0, :, cut], w1.at[:, cut], sems.at[base + 2 * c]))
        copies.append(pltpu.make_async_copy(w2_h.at[0, cut, :], w2.at[cut, :], sems.at[base + 2 * c + 1]))
    @pl.when(section < 2)
    def _():
        for copy in copies:
            copy.start()
        for copy in copies[:base]:
            copy.wait()

    @pl.when(section == 0)
    def _():
        tokens = TILE * HALF
        for k, v in enumerate(embed_rows(lat, inp, pos, (0, TILE - STRIDE), half)):
            acc[k * tokens : (k + 1) * tokens] = v
        norm[...] = normalise(acc[...], gain_ref[...])

    for c in range(chunks):
        cut = pl.ds(c * size, size)

        @pl.when(section < 2)
        def _():
            copies[base + 2 * c].wait()
            copies[base + 2 * c + 1].wait()

        @pl.when(section == 0)
        def _():
            h = gelu(jnp.dot(norm[...], w1[:, cut], preferred_element_type=F32)).astype(BF16)
            acc[...] += jnp.dot(h, w2[cut, :], preferred_element_type=F32)

    @pl.when(section == 0)
    def _():
        y[...] = acc[...].astype(BF16)

def table_kernel(anchors, out):
    a = anchors[...]
    column = lax.broadcasted_iota(jnp.int32, out.shape, 1) * STRIDE
    upper = lax.broadcasted_iota(jnp.int32, out.shape, 0) == 1
    table = jnp.where(upper, -1, 0)
    for k in range(a.shape[0]):
        row = jnp.broadcast_to(a[k : k + 1, 0:1], out.shape)
        here = jnp.broadcast_to(a[k : k + 1, 1:2], out.shape) == column
        table = jnp.where(here, jnp.where(upper, jnp.maximum(table, row), table + row), table)
    out[...] = table


def join_kernel(*refs):
    *tables, out = refs
    upper = lax.broadcasted_iota(jnp.int32, out.shape, 0) == 1
    total = tables[0][...]
    for table in tables[1:]:
        other = table[...]
        total = jnp.where(upper, jnp.maximum(total, other), total + other)
    out[...] = total


def tick_kernel(roles, outs, names, *refs):
    at = dict(zip(names, refs))
    section, slab = lax.axis_index("section"), lax.axis_index("win")
    parity = lax.rem(slab, 2)
    norm, acc = at["norm"], at["acc"]
    w1, w2 = at.get("new_w1", at["w1"]), at.get("new_w2", at["w2"])
    dim, hidden = w1.shape
    tokens = TILE * HALF

    def anchor_of(part):
        if part < 2:
            return part * STRIDE
        table = at["table"][...]
        slabs = table.shape[1]
        odd = lax.rem(slab + slabs - 1 + parity, slabs)
        here = lax.broadcasted_iota(jnp.int32, table.shape, 1) == odd
        upper = lax.broadcasted_iota(jnp.int32, table.shape, 0) == 1
        top = jnp.sum(jnp.where(here & upper, table, 0))
        return top if part == 2 else jnp.sum(jnp.where(here & ~upper, table, 0)) - top

    def rows_of(s):
        return pl.ds(0, tokens * len(roles[s]))

    def taken(name, s):
        size = tokens * len(roles[s])
        return at[name][pl.ds(tokens * (roles[s][0] % 2) % at[name].shape[0], size)]

    loads = [name for name in names if name.endswith("_h")]
    if loads:
        moves = []
        for k, name in enumerate(loads):
            whole, kept = at[name], at["new_" + name[:-2]]
            moves.append(
                pltpu.make_async_copy(whole.at[0] if whole.ndim > 2 else whole, kept, at["sems"].at[k])
            )

        @pl.when(section >= 2)
        def _():
            for move in moves[:3]:
                move.start()

            @pl.when(section == 3)
            def _():
                for move in moves[3:]:
                    move.start()

            for move in moves[:3]:
                move.wait()

        @pl.when(section == 3)
        def _():
            for move in moves[3:]:
                move.wait()

    if roles[0]:

        @pl.when(section == 0)
        def _():
            half = parity if roles[0][0] < 2 else 1 - parity
            where = [anchor_of(p) for p in roles[0]]
            for k, v in enumerate(embed_rows(at["lat"], at["inp"], at["pos"], where, half)):
                acc[k * tokens : (k + 1) * tokens] = v

    if "pass0" in at:

        @pl.when(section == 0)
        def _():
            at["y"][...] = at["pass0"][...]

    if roles[1]:

        @pl.when(section == 1)
        def _():
            acc[rows_of(1)] = taken("near1", 1).astype(F32)

    if roles[2]:

        @pl.when(section == 2)
        def _():
            acc[rows_of(2)] = taken("far2", 2).astype(F32)

    if roles[3]:

        @pl.when(section == 3)
        def _():
            acc[rows_of(3)] = jnp.dot(
                taken("near3", 3), at["skip"][:dim, :], preferred_element_type=F32
            ) + jnp.dot(taken("first3", 3), at["skip"][dim:, :], preferred_element_type=F32)

    for count in (1, 2):
        busy = [s for s in range(4) if len(roles[s]) == count]
        if not busy:
            continue
        assert busy == list(range(busy[0], busy[-1] + 1))

        @pl.when((section >= busy[0]) & (section <= busy[-1]))
        def _():
            rows = pl.ds(0, tokens * count)
            norm[rows] = normalise(acc[rows], at["gain"][...])
            size = hidden // 2

            def piece(c):
                cut = pl.ds(c * size, size)
                h = gelu(jnp.dot(norm[rows], w1[:, cut], preferred_element_type=F32)).astype(BF16)
                acc[rows] += jnp.dot(h, w2[cut, :], preferred_element_type=F32)

            if count == 1:
                piece(0)
                piece(1)
            else:
                pl.loop(0, 2)(piece)
            for name in sorted({outs[s] for s in busy if s < 3}):
                at[name][...] = acc[rows].astype(BF16)

    if roles[3]:
        totals = at["totals"]

        @pl.when(section == 3)
        def _():
            deep = acc[rows_of(3)].astype(BF16)
            noise = jnp.dot(deep, at["outp"][...], preferred_element_type=F32)
            noise = noise.astype(BF16).astype(F32)
            noise = noise.reshape(len(roles[3]), TILE, HALF, noise.shape[-1])
            if roles[3][0] == 0:
                totals[...] = jnp.zeros(totals.shape, F32)
            else:
                totals[...] = at["sums"][...]
            for k, part in enumerate(roles[3]):
                rows = pl.ds(anchor_of(part), TILE)
                totals[rows] = totals[rows] + noise[k]
            if roles[3][-1] == 3:
                row = lax.broadcasted_iota(jnp.int32, totals.shape, 0)
                count = jnp.zeros(totals.shape, F32)
                for k in range(4):
                    a = anchor_of(k)
                    count += ((row >= a) & (row < a + TILE)).astype(F32)
                band = totals.shape[0] // 4
                for k in range(4):
                    rows = slice(k * band, (k + 1) * band)
                    at[f"band{k}"][...] = (totals[rows] / count[rows]).astype(BF16)


def per_device(
    latent, anchors, in_proj, pos_embed, section_w1, section_w2, section_gain, skip_w, out_proj
):
    section = lax.axis_index("section")
    slab = lax.axis_index("win")
    sections, slabs = lax.axis_size("section"), lax.axis_size("win")
    height, width, feat = latent.shape
    dim = in_proj.shape[1]
    hidden = section_w1.shape[2]
    tokens = TILE * HALF
    axes = ("section", "win")
    positions = pos_embed.reshape(TILE, 2, HALF, dim)

    def hop(value, *pairs):
        return lax.ppermute(
            value, axes, [(a * slabs + w, b * slabs + w) for a, b in pairs for w in range(slabs)]
        )

    def swap(value):
        return hop(value, (0, 1), (1, 0), (2, 3), (3, 2))

    vmem = pl.BlockSpec(memory_space=pltpu.VMEM)
    hbm = pl.BlockSpec(memory_space=pltpu.HBM)
    any_space = pl.BlockSpec(memory_space=pl.ANY)

    def small_call(kernel, *given):
        return pl.pallas_call(
            kernel,
            out_shape=jax.ShapeDtypeStruct((2, slabs), jnp.int32),
            in_specs=[vmem] * len(given),
            out_specs=vmem,
            compiler_params=pltpu.CompilerParams(vmem_limit_bytes=MIB),
        )(*given)

    tables = [small_call(table_kernel, anchors)]
    def join(stride, extent):
        pairs = [
            [(w, w + stride * ((w // stride + k) % extent - w // stride % extent)) for w in range(slabs)]
            for k in range(1, extent)
        ]
        others = [lax.ppermute(tables[-1], "win", p) for p in pairs]
        tables.append(small_call(join_kernel, tables[-1], *others))

    join(*ROUNDS[0])

    chunks = 5

    def act(parts):
        return jax.ShapeDtypeStruct((parts * tokens, dim), BF16)

    def room(parts):
        return [pltpu.VMEM((parts * tokens, dim), BF16), pltpu.VMEM((parts * tokens, dim), F32)]

    def like(a, shape=None):
        return jax.ShapeDtypeStruct(shape or a.shape, a.dtype)

    def held(a, shape=None):
        return pltpu.VMEM(shape or a.shape, a.dtype)

    def pinned(a):
        return pltpu.with_memory_space_constraint(a, pltpu.VMEM)

    y0, lat, inp, pos, gain, w1, w2 = pl.pallas_call(
        functools.partial(load_kernel, chunks),
        out_shape=[
            act(2), held(latent), held(in_proj), held(positions), held(section_gain),
            held(section_w1, (dim, hidden)), held(section_w2, (hidden, dim)),
        ],
        in_specs=[hbm] * 6,
        out_specs=[vmem] * 7,
        scratch_shapes=room(2) + [pltpu.SemaphoreType.DMA((4 + 2 * chunks,))],
        compiler_params=pltpu.CompilerParams(vmem_limit_bytes=16 * MIB),
    )(
        *(
            pltpu.with_memory_space_constraint(a, pltpu.HBM)
            for a in (
                latent, in_proj, positions, section_gain, section_w1, section_w2
            )
        ),
    )

    lat, inp, pos, gain, w1, w2 = map(pinned, (lat, inp, pos, gain, w1, w2))
    held_now = dict(gain=gain, w1=w1, w2=w2)
    last_loads = dict(
        gain_h=section_gain, w1_h=section_w1, w2_h=section_w2, skip_h=skip_w, outp_h=out_proj
    )
    late = {}

    def tick(roles, outs, after=(), load={}, **extra):
        roles = [roles.get(s, ()) for s in range(4)]
        outs = [outs.get(s) for s in range(4)]
        given = {**held_now, **({k: late[k] for k in held_now} if late else {})}
        if any(p >= 2 for p in (*roles[0], *roles[3])):
            given["table"] = tables[-1]
        if roles[0]:
            given.update(lat=lat, inp=inp, pos=pos)
        if roles[3]:
            given.update(late)
        given.update(extra)
        specs = [vmem] * len(given) + [any_space] * len(after)
        if load:
            given.update(
                {k: pltpu.with_memory_space_constraint(a, pltpu.HBM) for k, a in load.items()}
            )
            specs += [hbm] * len(load)
        given.update({f"after{k}": a for k, a in enumerate(after)})
        made = {outs[s]: act(len(roles[s])) for s in range(3) if roles[s]}
        aliases = {}
        scratch = dict(zip(("norm", "acc"), room(max(map(len, roles)))))
        if load:
            made.update({"new_" + k[:-2]: held(a, a.shape[-2:]) for k, a in load.items()})
            aliases = {
                list(given).index(k): list(made).index("new_" + k) for k in held_now
            }
            scratch["sems"] = pltpu.SemaphoreType.DMA((len(load),))
        if roles[3] and roles[3][-1] == 3:
            for k in range(sections):
                made[f"band{k}"] = like(latent, (height // sections, *latent.shape[1:]))
            scratch["totals"] = pltpu.VMEM(latent.shape, F32)
        elif roles[3]:
            made["totals"] = jax.ShapeDtypeStruct(latent.shape, F32)
        results = pl.pallas_call(
            functools.partial(tick_kernel, roles, outs, [*given, *made, *scratch]),
            out_shape=list(made.values()),
            in_specs=specs,
            out_specs=[vmem] * len(made),
            scratch_shapes=list(scratch.values()),
            input_output_aliases=aliases,
            cost_estimate=pl.CostEstimate(
                flops=COST * sum(map(len, roles)) * 4 * tokens * dim * hidden,
                bytes_accessed=MIB,
                transcendentals=0,
            ),
            compiler_params=pltpu.CompilerParams(vmem_limit_bytes=16 * MIB),
        )(*given.values())
        return dict(zip(made, results))

    y0, _ = lax.optimization_barrier((y0, tables[1]))
    near01 = swap(y0)
    first01 = hop(y0, (0, 3))
    k1 = tick({1: (0, 1)}, {1: "y"}, near1=near01, load=last_loads)
    late.update({name[:-2]: pinned(k1["new_" + name[:-2]]) for name in last_loads})
    far01 = hop(k1["y"], (1, 2))
    tables[1], _ = lax.optimization_barrier((tables[1], k1["y"]))
    for stride, extent in ROUNDS[1:]:
        join(stride, extent)
    f2 = tick({0: (2,)}, {0: "y"}, after=[first01, far01])["y"]
    near2 = swap(f2)
    f3 = tick({0: (3,)}, {0: "y"}, after=[f2])["y"]
    s2 = tick({1: (2,)}, {1: "y"}, near1=near2, pass0=f2, after=[f3])["y"]
    cross2 = hop(s2, (1, 2), (0, 3))
    near3 = swap(f3)
    t01 = tick({2: (0, 1)}, {2: "t"}, far2=far01, after=[s2])["t"]
    third01 = swap(t01)
    s3 = tick({1: (3,)}, {1: "y"}, near1=near3, pass0=f3, after=[t01])["y"]
    cross3 = hop(s3, (1, 2), (0, 3))
    d01 = tick({3: (0, 1)}, {}, near3=third01, first3=first01, after=[s3])["totals"]
    t2 = tick({2: (2,)}, {2: "t"}, far2=cross2, after=[d01])["t"]
    third2 = swap(t2)
    t3 = tick({2: (3,)}, {2: "t"}, far2=cross3, after=[t2])["t"]
    d2 = tick({3: (2,)}, {}, near3=third2, first3=cross2, sums=d01)["totals"]
    t3, _ = lax.optimization_barrier((t3, d2))
    third3 = swap(t3)
    bands = tick({3: (3,)}, {}, near3=third3, first3=cross3, sums=d2)
    sent = [hop(bands[f"band{s}"], (3, s)) for s in range(3)]
    result = bands["band3"]
    for s in range(3):
        result = jnp.where(section == s, sent[s], result)
    return result


def solution(mesh):
    placed = (
        P(None, "win", None),
        P("win", None),
        P(),
        P(),
        P("section", None, None),
        P("section", None, None),
        P("section", None),
        P(),
        P(),
    )
    return jax.shard_map(
        per_device, mesh=mesh, in_specs=placed, out_specs=P("section", "win", None), check_vma=False
    )
```

profile of v0, /device:TPU:0, one launch (start us, length us, event | category | flops | bytes accessed | tf_op | source)
XLA Modules:
  0.0 69.0 jit_solution(9739217051975600115)
XLA Ops:
  0.8 2.1 %collective-permute-start = (s32[2,32]{1,0:T(2,128)S(1)}, s32[2,32]{1,0:T(2,128)S(1)}, u32[]{:S(2)}, u32[]{:S(2)}) collective-permute-start(s32[2,32]{1,0:T(2,128)S(1)} %shard_map.92.refs_0_), channel_id=1, source_target_pairs={{0,16},{1,17},{2,18},{3,19},{4,20},{5,21},{6,22},{7,23},{8,24},{9,... | collective-permute-start | bytes 776 | tf_op jit(solution)/shard_map/ppermute | solution.py:287
  2.9 7.4 %shard_map.91 = (bf16[256,1280]{1,0:T(8,128)(2,1)S(1)}, bf16[24,8,256]{2,1,0:T(8,128)(2,1)S(1)}, bf16[256,1280]{1,0:T(8,128)(2,1)S(1)}, bf16[16,2,8,1280]{3,2,1,...) custom-call(bf16[24,8,256]{2,1,0:T(8,128)(2,1)} %lat_h.1, ...), custom_call_target="tpu_custom_call" | custom-call | tf_op jit(solution)/shard_map/pallas_call | solution.py:309
  10.4 1.3 %collective-permute-start.8 = (bf16[256,1280]{1,0:T(8,128)(2,1)S(1)}, bf16[256,1280]{1,0:T(8,128)(2,1)S(1)}, u32[]{:S(2)}, u32[]{:S(2)}) collective-permute-start(bf16[256,1280]{1,0:T(8,128)(2,1)S(1)} %get-tuple-element.29), channel_id=1, source_target_pairs={{0,96},{1,97},{2,98},{3,99},{4,100},{5,101},{6,102},{7,103},{8,104... | collective-permute-start | bytes 1966088 | tf_op jit(solution)/shard_map/ppermute | solution.py:261
  11.7 0.7 %collective-permute-done.1.refs_3_ = bf16[256,1280]{1,0:T(8,128)(2,1)S(1)} collective-permute-done((bf16[256,1280]{1,0:T(8,128)(2,1)S(1)}, bf16[256,1280]{1,0:T(8,128)(2,1)S(1)}, u32[]{:S(2)}, u32[]{:S(2)}) %collective-permute-start.1) | collective-permute-done | bytes 655392 | tf_op jit(solution)/shard_map/ppermute | solution.py:261
  13.2 1.6 %collective-permute-start.2 = (s32[2,32]{1,0:T(2,128)S(1)}, s32[2,32]{1,0:T(2,128)S(1)}, u32[]{:S(2)}, u32[]{:S(2)}) collective-permute-start(s32[2,32]{1,0:T(2,128)S(1)} %shard_map.93.refs_0_), channel_id=1, source_target_pairs={{0,1},{1,2},{2,3},{3,0},{4,5},{5,6},{6,7},{7,4},{8,9},{9,10},{10,1... | collective-permute-start | bytes 776 | tf_op jit(solution)/shard_map/ppermute | solution.py:287
  14.8 2.7 %collective-permute-start.3 = (s32[2,32]{1,0:T(2,128)S(1)}, s32[2,32]{1,0:T(2,128)S(1)}, u32[]{:S(2)}, u32[]{:S(2)}) collective-permute-start(s32[2,32]{1,0:T(2,128)S(1)} %shard_map.93.refs_0_), channel_id=1, source_target_pairs={{0,2},{1,3},{2,0},{3,1},{4,6},{5,7},{6,4},{7,5},{8,10},{9,11},{10,... | collective-permute-start | bytes 776 | tf_op jit(solution)/shard_map/ppermute | solution.py:287
  17.5 1.4 %collective-permute-start.4 = (s32[2,32]{1,0:T(2,128)S(1)}, s32[2,32]{1,0:T(2,128)S(1)}, u32[]{:S(2)}, u32[]{:S(2)}) collective-permute-start(s32[2,32]{1,0:T(2,128)S(1)} %shard_map.93.refs_0_), channel_id=1, source_target_pairs={{0,3},{1,0},{2,1},{3,2},{4,7},{5,4},{6,5},{7,6},{8,11},{9,8},{10,9... | collective-permute-start | bytes 776 | tf_op jit(solution)/shard_map/ppermute | solution.py:287
  18.9 0.9 %collective-permute-done.3.refs_2_ = s32[2,32]{1,0:T(2,128)S(1)} collective-permute-done((s32[2,32]{1,0:T(2,128)S(1)}, s32[2,32]{1,0:T(2,128)S(1)}, u32[]{:S(2)}, u32[]{:S(2)}) %collective-permute-start.3) | collective-permute-done | bytes 288 | tf_op jit(solution)/shard_map/ppermute | solution.py:287
  19.8 1.2 %collective-permute-done.4.refs_3_ = s32[2,32]{1,0:T(2,128)S(1)} collective-permute-done((s32[2,32]{1,0:T(2,128)S(1)}, s32[2,32]{1,0:T(2,128)S(1)}, u32[]{:S(2)}, u32[]{:S(2)}) %collective-permute-start.4) | collective-permute-done | bytes 288 | tf_op jit(solution)/shard_map/ppermute | solution.py:287
  21.1 1.6 %collective-permute-start.5 = (s32[2,32]{1,0:T(2,128)S(1)}, s32[2,32]{1,0:T(2,128)S(1)}, u32[]{:S(2)}, u32[]{:S(2)}) collective-permute-start(s32[2,32]{1,0:T(2,128)S(1)} %shard_map.95.refs_0_), channel_id=1, source_target_pairs={{0,4},{1,5},{2,6},{3,7},{4,8},{5,9},{6,10},{7,11},{8,12},{9,13},{1... | collective-permute-start | bytes 776 | tf_op jit(solution)/shard_map/ppermute | solution.py:287
  22.7 2.9 %collective-permute-start.6 = (s32[2,32]{1,0:T(2,128)S(1)}, s32[2,32]{1,0:T(2,128)S(1)}, u32[]{:S(2)}, u32[]{:S(2)}) collective-permute-start(s32[2,32]{1,0:T(2,128)S(1)} %shard_map.95.refs_0_), channel_id=1, source_target_pairs={{0,8},{1,9},{2,10},{3,11},{4,12},{5,13},{6,14},{7,15},{8,0},{9,1},... | collective-permute-start | bytes 776 | tf_op jit(solution)/shard_map/ppermute | solution.py:287
  25.6 1.3 %collective-permute-start.7 = (s32[2,32]{1,0:T(2,128)S(1)}, s32[2,32]{1,0:T(2,128)S(1)}, u32[]{:S(2)}, u32[]{:S(2)}) collective-permute-start(s32[2,32]{1,0:T(2,128)S(1)} %shard_map.95.refs_0_), channel_id=1, source_target_pairs={{0,12},{1,13},{2,14},{3,15},{4,0},{5,1},{6,2},{7,3},{8,4},{9,5},{1... | collective-permute-start | bytes 776 | tf_op jit(solution)/shard_map/ppermute | solution.py:287
  27.0 0.8 %collective-permute-done.6.refs_2_ = s32[2,32]{1,0:T(2,128)S(1)} collective-permute-done((s32[2,32]{1,0:T(2,128)S(1)}, s32[2,32]{1,0:T(2,128)S(1)}, u32[]{:S(2)}, u32[]{:S(2)}) %collective-permute-start.6) | collective-permute-done | bytes 288 | tf_op jit(solution)/shard_map/ppermute | solution.py:287
  27.8 1.4 %collective-permute-done.7.refs_3_ = s32[2,32]{1,0:T(2,128)S(1)} collective-permute-done((s32[2,32]{1,0:T(2,128)S(1)}, s32[2,32]{1,0:T(2,128)S(1)}, u32[]{:S(2)}, u32[]{:S(2)}) %collective-permute-start.7) | collective-permute-done | bytes 288 | tf_op jit(solution)/shard_map/ppermute | solution.py:287
  29.2 2.5 %shard_map.97.refs_7_.refs_4_ = bf16[128,1280]{1,0:T(8,128)(2,1)S(1)} custom-call(f32[1,1280]{1,0:T(1,128)S(1)} %get-tuple-element.30.refs_0_, bf16[1280,2560]{1,0:T(8,128)(2,1)S(1)} %get-tuple-element.31.refs_1_, bf16[2560,1280]{1,0:T(8,128)(2,1)S(1)} %get-tuple-element.32.refs_2_, s32[2,32]{1,0:T(2,128)S(1)} %shard_map.96.refs_3_, ...), custom_call_target="tpu_custom_call" | custom-call | flops 26843545600 | bytes 1048576 | tf_op jit(solution)/shard_map/pallas_call | solution.py:368
  31.9 2.7 %shard_map.98.refs_5_.refs_4_ = bf16[128,1280]{1,0:T(8,128)(2,1)S(1)} custom-call(f32[1,1280]{1,0:T(1,128)S(1)} %get-tuple-element.30.refs_0_, bf16[1280,2560]{1,0:T(8,128)(2,1)S(1)} %get-tuple-element.31.refs_1_, bf16[2560,1280]{1,0:T(8,128)(2,1)S(1)} %get-tuple-element.32.refs_2_, s32[2,32]{1,0:T(2,128)S(1)} %shard_map.96.refs_3_, ...), custom_call_target="tpu_custom_call" | custom-call | flops 26843545600 | bytes 1048576 | tf_op jit(solution)/shard_map/pallas_call | solution.py:368
  34.7 1.3 %collective-permute-start.13 = (bf16[128,1280]{1,0:T(8,128)(2,1)S(1)}, bf16[128,1280]{1,0:T(8,128)(2,1)S(1)}, u32[]{:S(2)}, u32[]{:S(2)}) collective-permute-start(bf16[128,1280]{1,0:T(8,128)(2,1)S(1)} %shard_map.99.refs_4_), channel_id=1, source_target_pairs={{32,64},{33,65},{34,66},{35,67},{36,68},{37,69},{38,70},{39,71},{4... | collective-permute-start | bytes 983048 | tf_op jit(solution)/shard_map/ppermute | solution.py:261
  36.1 2.7 %collective-permute-start.14 = (bf16[256,1280]{1,0:T(8,128)(2,1)S(1)}, bf16[256,1280]{1,0:T(8,128)(2,1)S(1)}, u32[]{:S(2)}, u32[]{:S(2)}) collective-permute-start(bf16[256,1280]{1,0:T(8,128)(2,1)S(1)} %shard_map.100.refs_5_), channel_id=1, source_target_pairs={{0,32},{1,33},{2,34},{3,35},{4,36},{5,37},{6,38},{7,39},{8,40},{9,... | collective-permute-start | bytes 1966088 | tf_op jit(solution)/shard_map/ppermute | solution.py:261
  38.9 3.5 %collective-permute-start.12 = (bf16[128,1280]{1,0:T(8,128)(2,1)S(1)}, bf16[128,1280]{1,0:T(8,128)(2,1)S(1)}, u32[]{:S(2)}, u32[]{:S(2)}) collective-permute-start(bf16[128,1280]{1,0:T(8,128)(2,1)S(1)} %shard_map.101.refs_7_), channel_id=1, source_target_pairs={{32,64},{33,65},{34,66},{35,67},{36,68},{37,69},{38,70},{39,71},{4... | collective-permute-start | bytes 983048 | tf_op jit(solution)/shard_map/ppermute | solution.py:261
  42.7 2.1 %collective-permute-start.15 = (bf16[128,1280]{1,0:T(8,128)(2,1)S(1)}, bf16[128,1280]{1,0:T(8,128)(2,1)S(1)}, u32[]{:S(2)}, u32[]{:S(2)}) collective-permute-start(bf16[128,1280]{1,0:T(8,128)(2,1)S(1)} %shard_map.103.refs_4_), channel_id=1, source_target_pairs={{0,32},{1,33},{2,34},{3,35},{4,36},{5,37},{6,38},{7,39},{8,40},{9,... | collective-permute-start | bytes 983048 | tf_op jit(solution)/shard_map/ppermute | solution.py:261
  44.8 5.7 %collective-permute-done.12.refs_3_.refs_7_ = bf16[128,1280]{1,0:T(8,128)(2,1)S(1)} collective-permute-done((bf16[128,1280]{1,0:T(8,128)(2,1)S(1)}, bf16[128,1280]{1,0:T(8,128)(2,1)S(1)}, u32[]{:S(2)}, u32[]{:S(2)}) %collective-permute-start.12) | collective-permute-done | bytes 327712 | tf_op jit(solution)/shard_map/ppermute | solution.py:261
  51.3 1.3 %collective-permute-done.16.refs_6_ = bf16[128,1280]{1,0:T(8,128)(2,1)S(1)} collective-permute-done((bf16[128,1280]{1,0:T(8,128)(2,1)S(1)}, bf16[128,1280]{1,0:T(8,128)(2,1)S(1)}, u32[]{:S(2)}, u32[]{:S(2)}) %collective-permute-start.16) | collective-permute-done | bytes 327712 | tf_op jit(solution)/shard_map/ppermute | solution.py:261
  53.9 1.3 %collective-permute-start.19 = (bf16[6,8,256]{2,1,0:T(8,128)(2,1)S(1)}, bf16[6,8,256]{2,1,0:T(8,128)(2,1)S(1)}, u32[]{:S(2)}, u32[]{:S(2)}) collective-permute-start(bf16[6,8,256]{2,1,0:T(8,128)(2,1)S(1)} %get-tuple-element.43), channel_id=1, source_target_pairs={{96,0},{97,1},{98,2},{99,3},{100,4},{101,5},{102,6},{103,7},{104,8... | collective-permute-start | bytes 73736 | tf_op jit(solution)/shard_map/ppermute | solution.py:261
  55.2 13.2 %collective-permute-done.19 = bf16[6,8,256]{2,1,0:T(8,128)(2,1)S(1)} collective-permute-done((bf16[6,8,256]{2,1,0:T(8,128)(2,1)S(1)}, bf16[6,8,256]{2,1,0:T(8,128)(2,1)S(1)}, u32[]{:S(2)}, u32[]{:S(2)}) %collective-permute-start.19) | collective-permute-done | bytes 24608 | tf_op jit(solution)/shard_map/ppermute | solution.py:261
  (39 shorter events, 4.9 us)
Async XLA Ops:
  0.0 0.7 copy-start.2
  0.8 9.4 %collective-permute-start = (s32[2,32]{1,0:T(2,128)S(1)}, s32[2,32]{1,0:T(2,128)S(1)}, u32[]{:S(2)}, u32[]{:S(2)}) collective-permute-start(s32[2,32]{1,0:T(2,128)S(1)} %shard_map.92.refs_0_), channel_id=1, source_target_pairs={{0,16},{1,17},{2,18},{3,19},{4,20},{5,21},{6,22},{7,23},{8,24},{9,... | collective-permute-start | bytes 776 | tf_op jit(solution)/shard_map/ppermute | solution.py:287
  10.3 2.2 %collective-permute-start.1 = (bf16[256,1280]{1,0:T(8,128)(2,1)S(1)}, bf16[256,1280]{1,0:T(8,128)(2,1)S(1)}, u32[]{:S(2)}, u32[]{:S(2)}) collective-permute-start(bf16[256,1280]{1,0:T(8,128)(2,1)S(1)} %get-tuple-element.29), channel_id=1, source_target_pairs={{0,32},{1,33},{2,34},{3,35},{4,36},{5,37},{6,38},{7,39},{8,40},{9,... | collective-permute-start | bytes 1966088 | tf_op jit(solution)/shard_map/ppermute | solution.py:261
  10.4 18.9 %collective-permute-start.8 = (bf16[256,1280]{1,0:T(8,128)(2,1)S(1)}, bf16[256,1280]{1,0:T(8,128)(2,1)S(1)}, u32[]{:S(2)}, u32[]{:S(2)}) collective-permute-start(bf16[256,1280]{1,0:T(8,128)(2,1)S(1)} %get-tuple-element.29), channel_id=1, source_target_pairs={{0,96},{1,97},{2,98},{3,99},{4,100},{5,101},{6,102},{7,103},{8,104... | collective-permute-start | bytes 1966088 | tf_op jit(solution)/shard_map/ppermute | solution.py:261
  12.5 16.7 %collective-permute-start.9 = (bf16[256,1280]{1,0:T(8,128)(2,1)S(1)}, bf16[256,1280]{1,0:T(8,128)(2,1)S(1)}, u32[]{:S(2)}, u32[]{:S(2)}) collective-permute-start(bf16[256,1280]{1,0:T(8,128)(2,1)S(1)} %get-tuple-element.33), channel_id=1, source_target_pairs={{32,64},{33,65},{34,66},{35,67},{36,68},{37,69},{38,70},{39,71},{4... | collective-permute-start | bytes 1966088 | tf_op jit(solution)/shard_map/ppermute | solution.py:261
  13.2 5.7 %collective-permute-start.2 = (s32[2,32]{1,0:T(2,128)S(1)}, s32[2,32]{1,0:T(2,128)S(1)}, u32[]{:S(2)}, u32[]{:S(2)}) collective-permute-start(s32[2,32]{1,0:T(2,128)S(1)} %shard_map.93.refs_0_), channel_id=1, source_target_pairs={{0,1},{1,2},{2,3},{3,0},{4,5},{5,6},{6,7},{7,4},{8,9},{9,10},{10,1... | collective-permute-start | bytes 776 | tf_op jit(solution)/shard_map/ppermute | solution.py:287
  14.8 5.1 %collective-permute-start.3 = (s32[2,32]{1,0:T(2,128)S(1)}, s32[2,32]{1,0:T(2,128)S(1)}, u32[]{:S(2)}, u32[]{:S(2)}) collective-permute-start(s32[2,32]{1,0:T(2,128)S(1)} %shard_map.93.refs_0_), channel_id=1, source_target_pairs={{0,2},{1,3},{2,0},{3,1},{4,6},{5,7},{6,4},{7,5},{8,10},{9,11},{10,... | collective-permute-start | bytes 776 | tf_op jit(solution)/shard_map/ppermute | solution.py:287
  17.5 3.6 %collective-permute-start.4 = (s32[2,32]{1,0:T(2,128)S(1)}, s32[2,32]{1,0:T(2,128)S(1)}, u32[]{:S(2)}, u32[]{:S(2)}) collective-permute-start(s32[2,32]{1,0:T(2,128)S(1)} %shard_map.93.refs_0_), channel_id=1, source_target_pairs={{0,3},{1,0},{2,1},{3,2},{4,7},{5,4},{6,5},{7,6},{8,11},{9,8},{10,9... | collective-permute-start | bytes 776 | tf_op jit(solution)/shard_map/ppermute | solution.py:287
  21.1 5.9 %collective-permute-start.5 = (s32[2,32]{1,0:T(2,128)S(1)}, s32[2,32]{1,0:T(2,128)S(1)}, u32[]{:S(2)}, u32[]{:S(2)}) collective-permute-start(s32[2,32]{1,0:T(2,128)S(1)} %shard_map.95.refs_0_), channel_id=1, source_target_pairs={{0,4},{1,5},{2,6},{3,7},{4,8},{5,9},{6,10},{7,11},{8,12},{9,13},{1... | collective-permute-start | bytes 776 | tf_op jit(solution)/shard_map/ppermute | solution.py:287
  22.7 5.1 %collective-permute-start.6 = (s32[2,32]{1,0:T(2,128)S(1)}, s32[2,32]{1,0:T(2,128)S(1)}, u32[]{:S(2)}, u32[]{:S(2)}) collective-permute-start(s32[2,32]{1,0:T(2,128)S(1)} %shard_map.95.refs_0_), channel_id=1, source_target_pairs={{0,8},{1,9},{2,10},{3,11},{4,12},{5,13},{6,14},{7,15},{8,0},{9,1},... | collective-permute-start | bytes 776 | tf_op jit(solution)/shard_map/ppermute | solution.py:287
  25.6 3.6 %collective-permute-start.7 = (s32[2,32]{1,0:T(2,128)S(1)}, s32[2,32]{1,0:T(2,128)S(1)}, u32[]{:S(2)}, u32[]{:S(2)}) collective-permute-start(s32[2,32]{1,0:T(2,128)S(1)} %shard_map.95.refs_0_), channel_id=1, source_target_pairs={{0,12},{1,13},{2,14},{3,15},{4,0},{5,1},{6,2},{7,3},{8,4},{9,5},{1... | collective-permute-start | bytes 776 | tf_op jit(solution)/shard_map/ppermute | solution.py:287
  29.2 2.7 %copy-start = (s32[2,32]{1,0:T(2,128)}, s32[2,32]{1,0:T(2,128)S(1)}, u32[]{:S(2)}) copy-start(s32[2,32]{1,0:T(2,128)S(1)} %shard_map.96.refs_3_) | copy-start | bytes 772
  31.8 2.9 %collective-permute-start.11 = (bf16[128,1280]{1,0:T(8,128)(2,1)S(1)}, bf16[128,1280]{1,0:T(8,128)(2,1)S(1)}, u32[]{:S(2)}, u32[]{:S(2)}) collective-permute-start(bf16[128,1280]{1,0:T(8,128)(2,1)S(1)} %shard_map.97.refs_7_.refs_4_), channel_id=1, source_target_pairs={{0,32},{1,33},{2,34},{3,35},{4,36},{5,37},{6,38},{7,39},{8,40},{9,... | collective-permute-start | bytes 983048 | tf_op jit(solution)/shard_map/ppermute | solution.py:261
  34.6 4.2 %collective-permute-start.10 = (bf16[128,1280]{1,0:T(8,128)(2,1)S(1)}, bf16[128,1280]{1,0:T(8,128)(2,1)S(1)}, u32[]{:S(2)}, u32[]{:S(2)}) collective-permute-start(bf16[128,1280]{1,0:T(8,128)(2,1)S(1)} %shard_map.98.refs_5_.refs_4_), channel_id=1, source_target_pairs={{0,32},{1,33},{2,34},{3,35},{4,36},{5,37},{6,38},{7,39},{8,40},{9,... | collective-permute-start | bytes 983048 | tf_op jit(solution)/shard_map/ppermute | solution.py:261
  34.7 7.9 %collective-permute-start.13 = (bf16[128,1280]{1,0:T(8,128)(2,1)S(1)}, bf16[128,1280]{1,0:T(8,128)(2,1)S(1)}, u32[]{:S(2)}, u32[]{:S(2)}) collective-permute-start(bf16[128,1280]{1,0:T(8,128)(2,1)S(1)} %shard_map.99.refs_4_), channel_id=1, source_target_pairs={{32,64},{33,65},{34,66},{35,67},{36,68},{37,69},{38,70},{39,71},{4... | collective-permute-start | bytes 983048 | tf_op jit(solution)/shard_map/ppermute | solution.py:261
  36.1 6.3 %collective-permute-start.14 = (bf16[256,1280]{1,0:T(8,128)(2,1)S(1)}, bf16[256,1280]{1,0:T(8,128)(2,1)S(1)}, u32[]{:S(2)}, u32[]{:S(2)}) collective-permute-start(bf16[256,1280]{1,0:T(8,128)(2,1)S(1)} %shard_map.100.refs_5_), channel_id=1, source_target_pairs={{0,32},{1,33},{2,34},{3,35},{4,36},{5,37},{6,38},{7,39},{8,40},{9,... | collective-permute-start | bytes 1966088 | tf_op jit(solution)/shard_map/ppermute | solution.py:261
  38.9 11.7 %collective-permute-start.12 = (bf16[128,1280]{1,0:T(8,128)(2,1)S(1)}, bf16[128,1280]{1,0:T(8,128)(2,1)S(1)}, u32[]{:S(2)}, u32[]{:S(2)}) collective-permute-start(bf16[128,1280]{1,0:T(8,128)(2,1)S(1)} %shard_map.101.refs_7_), channel_id=1, source_target_pairs={{32,64},{33,65},{34,66},{35,67},{36,68},{37,69},{38,70},{39,71},{4... | collective-permute-start | bytes 983048 | tf_op jit(solution)/shard_map/ppermute | solution.py:261
  42.7 7.8 %copy-start.1 = (s32[2,32]{1,0:T(2,128)S(1)}, s32[2,32]{1,0:T(2,128)}, u32[]{:S(2)}) copy-start(s32[2,32]{1,0:T(2,128)} %copy-done) | copy-start | bytes 772
  42.7 7.8 %collective-permute-start.15 = (bf16[128,1280]{1,0:T(8,128)(2,1)S(1)}, bf16[128,1280]{1,0:T(8,128)(2,1)S(1)}, u32[]{:S(2)}, u32[]{:S(2)}) collective-permute-start(bf16[128,1280]{1,0:T(8,128)(2,1)S(1)} %shard_map.103.refs_4_), channel_id=1, source_target_pairs={{0,32},{1,33},{2,34},{3,35},{4,36},{5,37},{6,38},{7,39},{8,40},{9,... | collective-permute-start | bytes 983048 | tf_op jit(solution)/shard_map/ppermute | solution.py:261
  50.6 2.0 %collective-permute-start.16 = (bf16[128,1280]{1,0:T(8,128)(2,1)S(1)}, bf16[128,1280]{1,0:T(8,128)(2,1)S(1)}, u32[]{:S(2)}, u32[]{:S(2)}) collective-permute-start(bf16[128,1280]{1,0:T(8,128)(2,1)S(1)} %shard_map.104), channel_id=1, source_target_pairs={{0,32},{1,33},{2,34},{3,35},{4,36},{5,37},{6,38},{7,39},{8,40},{9,... | collective-permute-start | bytes 983048 | tf_op jit(solution)/shard_map/ppermute | solution.py:261
  52.5 2.6 %collective-permute-start.17 = (bf16[6,8,256]{2,1,0:T(8,128)(2,1)S(1)}, bf16[6,8,256]{2,1,0:T(8,128)(2,1)S(1)}, u32[]{:S(2)}, u32[]{:S(2)}) collective-permute-start(bf16[6,8,256]{2,1,0:T(8,128)(2,1)S(1)} %get-tuple-element.41), channel_id=1, source_target_pairs={{96,64},{97,65},{98,66},{99,67},{100,68},{101,69},{102,70},{103,71... | collective-permute-start | bytes 73736 | tf_op jit(solution)/shard_map/ppermute | solution.py:261
  53.2 2.0 %collective-permute-start.18 = (bf16[6,8,256]{2,1,0:T(8,128)(2,1)S(1)}, bf16[6,8,256]{2,1,0:T(8,128)(2,1)S(1)}, u32[]{:S(2)}, u32[]{:S(2)}) collective-permute-start(bf16[6,8,256]{2,1,0:T(8,128)(2,1)S(1)} %get-tuple-element.42), channel_id=1, source_target_pairs={{96,32},{97,33},{98,34},{99,35},{100,36},{101,37},{102,38},{103,39... | collective-permute-start | bytes 73736 | tf_op jit(solution)/shard_map/ppermute | solution.py:261
  53.9 14.5 %collective-permute-start.19 = (bf16[6,8,256]{2,1,0:T(8,128)(2,1)S(1)}, bf16[6,8,256]{2,1,0:T(8,128)(2,1)S(1)}, u32[]{:S(2)}, u32[]{:S(2)}) collective-permute-start(bf16[6,8,256]{2,1,0:T(8,128)(2,1)S(1)} %get-tuple-element.43), channel_id=1, source_target_pairs={{96,0},{97,1},{98,2},{99,3},{100,4},{101,5},{102,6},{103,7},{104,8... | collective-permute-start | bytes 73736 | tf_op jit(solution)/shard_map/ppermute | solution.py:261
where the time goes:
time: 69.2 us; the launch traced here: 69 us
  starting transfers between devices  29 us (42%)
  waiting for transfers between devices  25.2 us (36%)
  Pallas kernels  13.1 us (19%)
    ppermute x13, waiting for transfers between devices, hop(): lax.ppermute(value, axes, [(a * slabs + w, b * slabs + w) for a, b in pai...  20.9 us
    ppermute x13, starting transfers between devices, hop(): lax.ppermute(value, axes, [(a * slabs + w, b * slabs + w) for a, b in pai...  15.3 us
    ppermute x7, starting transfers between devices, join(): others = [lax.ppermute(tables[-1], 'win', p) for p in pairs]  13.7 us
    pallas_call x1, Pallas kernels, per_device(): pl.pallas_call(functools.partial(load_kernel, chunks), out_shape=[act(2),...  7.35 us
    pallas_call x11, Pallas kernels, tick(): pl.pallas_call(functools.partial(tick_kernel, roles, outs, [*given, *made...  5.64 us
    ppermute x7, waiting for transfers between devices, join(): others = [lax.ppermute(tables[-1], 'win', p) for p in pairs]  4.36 us
  transfers between devices with their start and end apart: 20, of which 8 were waited for; matrix products, arithmetic and copies ran while one was open for 0% of the time, Pallas kernels for 15%

commit v1 on v0

--- a/solution.py
+++ b/solution.py
@@ -12,7 +12,7 @@
 HALF = TILE // 2
 ROUNDS = ((16, 2), (1, 4), (4, 4))
 MIB = 1 << 20
-COST = 16
+COST = 8
 F32 = jnp.float32
 BF16 = jnp.bfloat16
 
@@ -63,18 +63,18 @@
             acc[k * tokens : (k + 1) * tokens] = v
         norm[...] = normalise(acc[...], gain_ref[...])
 
-    for c in range(chunks):
-        cut = pl.ds(c * size, size)
-
-        @pl.when(section < 2)
-        def _():
-            copies[base + 2 * c].wait()
-            copies[base + 2 * c + 1].wait()
-
-        @pl.when(section == 0)
-        def _():
-            h = gelu(jnp.dot(norm[...], w1[:, cut], preferred_element_type=F32)).astype(BF16)
-            acc[...] += jnp.dot(h, w2[cut, :], preferred_element_type=F32)
+    @pl.when(section < 2)
+    def _():
+        @pl.loop(0, chunks)
+        def _(c):
+            cut = pl.ds(pl.multiple_of(c * size, size), size)
+            pltpu.make_async_copy(w1_h.at[0, :, cut], w1.at[:, cut], sems.at[base + 2 * c]).wait()
+            pltpu.make_async_copy(w2_h.at[0, cut, :], w2.at[cut, :], sems.at[base + 2 * c + 1]).wait()
+
+            @pl.when(section == 0)
+            def _():
+                h = gelu(jnp.dot(norm[...], w1[:, cut], preferred_element_type=F32)).astype(BF16)
+                acc[...] += jnp.dot(h, w2[cut, :], preferred_element_type=F32)
 
     @pl.when(section == 0)
     def _():
@@ -164,12 +164,6 @@
             where = [anchor_of(p) for p in roles[0]]
             for k, v in enumerate(embed_rows(at["lat"], at["inp"], at["pos"], where, half)):
                 acc[k * tokens : (k + 1) * tokens] = v
-
-    if "pass0" in at:
-
-        @pl.when(section == 0)
-        def _():
-            at["y"][...] = at["pass0"][...]
 
     if roles[1]:
 
@@ -290,9 +284,10 @@
     join(*ROUNDS[0])
 
     chunks = 5
+    flops = 4 * tokens * dim * hidden
 
     def act(parts):
-        return jax.ShapeDtypeStruct((parts * tokens, dim), BF16)
+        return pltpu.VMEM((parts * tokens, dim), BF16)
 
     def room(parts):
         return [pltpu.VMEM((parts * tokens, dim), BF16), pltpu.VMEM((parts * tokens, dim), F32)]
@@ -342,7 +337,7 @@
             given.update(lat=lat, inp=inp, pos=pos)
         if roles[3]:
             given.update(late)
-        given.update(extra)
+        given.update({k: pinned(a) for k, a in extra.items()})
         specs = [vmem] * len(given) + [any_space] * len(after)
         if load:
             given.update(
@@ -364,7 +359,7 @@
                 made[f"band{k}"] = like(latent, (height // sections, *latent.shape[1:]))
             scratch["totals"] = pltpu.VMEM(latent.shape, F32)
         elif roles[3]:
-            made["totals"] = jax.ShapeDtypeStruct(latent.shape, F32)
+            made["totals"] = pltpu.VMEM(latent.shape, F32)
         results = pl.pallas_call(
             functools.partial(tick_kernel, roles, outs, [*given, *made, *scratch]),
             out_shape=list(made.values()),
@@ -373,7 +368,7 @@
             scratch_shapes=list(scratch.values()),
             input_output_aliases=aliases,
             cost_estimate=pl.CostEstimate(
-                flops=COST * sum(map(len, roles)) * 4 * tokens * dim * hidden,
+                flops=COST * sum(map(len, roles)) * flops,
                 bytes_accessed=MIB,
                 transcendentals=0,
             ),
@@ -391,24 +386,26 @@
     for stride, extent in ROUNDS[1:]:
         join(stride, extent)
     f2 = tick({0: (2,)}, {0: "y"}, after=[first01, far01])["y"]
-    near2 = swap(f2)
-    f3 = tick({0: (3,)}, {0: "y"}, after=[f2])["y"]
-    s2 = tick({1: (2,)}, {1: "y"}, near1=near2, pass0=f2, after=[f3])["y"]
-    cross2 = hop(s2, (1, 2), (0, 3))
+    near2 = hop(f2, (0, 1))
+    first2 = hop(f2, (0, 3))
+    s2 = tick({1: (2,)}, {1: "y"}, near1=near2)["y"]
+    far2 = hop(s2, (1, 2))
+    f3 = tick({0: (3,)}, {0: "y"}, after=[s2])["y"]
     near3 = swap(f3)
-    t01 = tick({2: (0, 1)}, {2: "t"}, far2=far01, after=[s2])["t"]
+    first3 = hop(f3, (0, 3))
+    t01 = tick({2: (0, 1)}, {2: "t"}, far2=far01, after=[f3])["t"]
     third01 = swap(t01)
-    s3 = tick({1: (3,)}, {1: "y"}, near1=near3, pass0=f3, after=[t01])["y"]
-    cross3 = hop(s3, (1, 2), (0, 3))
+    s3 = tick({1: (3,)}, {1: "y"}, near1=near3, after=[t01])["y"]
+    far3 = hop(s3, (1, 2))
     d01 = tick({3: (0, 1)}, {}, near3=third01, first3=first01, after=[s3])["totals"]
-    t2 = tick({2: (2,)}, {2: "t"}, far2=cross2, after=[d01])["t"]
+    t2 = tick({2: (2,)}, {2: "t"}, far2=far2, after=[d01])["t"]
     third2 = swap(t2)
-    t3 = tick({2: (3,)}, {2: "t"}, far2=cross3, after=[t2])["t"]
-    d2 = tick({3: (2,)}, {}, near3=third2, first3=cross2, sums=d01)["totals"]
+    t3 = tick({2: (3,)}, {2: "t"}, far2=far3, after=[t2])["t"]
+    d2 = tick({3: (2,)}, {}, near3=third2, first3=first2, sums=d01)["totals"]
     t3, _ = lax.optimization_barrier((t3, d2))
     third3 = swap(t3)
-    bands = tick({3: (3,)}, {}, near3=third3, first3=cross3, sums=d2)
-    sent = [hop(bands[f"band{s}"], (3, s)) for s in range(3)]
+    bands = tick({3: (3,)}, {}, near3=third3, first3=first3, sums=d2)
+    sent = [hop(a, (3, s)) for s, a in enumerate(bands[f"band{k}"] for k in range(3))]
     result = bands["band3"]
     for s in range(3):
         result = jnp.where(section == s, sent[s], result)

time: 69.2 us -> 67.2 us (0.971)
  waiting for transfers between devices: 25.2 us -> 21.5 us
  starting transfers between devices: 29 us -> 31 us
    ppermute x13 -> x15, waiting for transfers between devices: 20.9 us -> 17.1 us  [hop(): lax.ppermute(value, axes, [(a * slabs + w, b * slabs + w) for a, b in pai...]
    ppermute x13 -> x15, starting transfers between devices: 15.3 us -> 17.3 us  [hop(): lax.ppermute(value, axes, [(a * slabs + w, b * slabs + w) for a, b in pai...]
  transfers between devices with their start and end apart: 20 -> 22, of which waited for: 8 -> 9; matrix products, arithmetic and copies ran while one was open for 0% -> 0% of each run, Pallas kernels for 15% -> 15%
where the time goes in v1:
time: 67.2 us; the launch traced here: 67 us
  starting transfers between devices  31 us (46%)
  waiting for transfers between devices  21.5 us (32%)
  Pallas kernels  12.9 us (19%)
  local copies, waits for them, and re-layouts  0.68 us (1%)
    ppermute x15, starting transfers between devices, hop(): lax.ppermute(value, axes, [(a * slabs + w, b * slabs + w) for a, b in pai...  17.3 us
    ppermute x15, waiting for transfers between devices, hop(): lax.ppermute(value, axes, [(a * slabs + w, b * slabs + w) for a, b in pai...  17.1 us
    ppermute x7, starting transfers between devices, join(): others = [lax.ppermute(tables[-1], 'win', p) for p in pairs]  13.7 us
    pallas_call x1, Pallas kernels, per_device(): pl.pallas_call(functools.partial(load_kernel, chunks), out_shape=[act(2),...  7.41 us
    pallas_call x11, Pallas kernels, tick(): pl.pallas_call(functools.partial(tick_kernel, roles, outs, [*given, *made...  5.39 us
    ppermute x7, waiting for transfers between devices, join(): others = [lax.ppermute(tables[-1], 'win', p) for p in pairs]  4.36 us
  transfers between devices with their start and end apart: 22, of which 9 were waited for; matrix products, arithmetic and copies ran while one was open for 0% of the time, Pallas kernels for 15%

profile of v1, /device:TPU:0, one launch (start us, length us, event | category | flops | bytes accessed | tf_op | source)
XLA Modules:
  0.0 67.0 jit_solution(13632662299893717530)
XLA Ops:
  0.8 2.1 %collective-permute-start = (s32[2,32]{1,0:T(2,128)S(1)}, s32[2,32]{1,0:T(2,128)S(1)}, u32[]{:S(2)}, u32[]{:S(2)}) collective-permute-start(s32[2,32]{1,0:T(2,128)S(1)} %shard_map.92.refs_0_), channel_id=1, source_target_pairs={{0,16},{1,17},{2,18},{3,19},{4,20},{5,21},{6,22},{7,23},{8,24},{9,... | collective-permute-start | bytes 776 | tf_op jit(solution)/shard_map/ppermute | solution.py:281
  2.9 7.4 %shard_map.91 = (bf16[256,1280]{1,0:T(8,128)(2,1)S(1)}, bf16[24,8,256]{2,1,0:T(8,128)(2,1)S(1)}, bf16[256,1280]{1,0:T(8,128)(2,1)S(1)}, bf16[16,2,8,1280]{3,2,1,...) custom-call(bf16[24,8,256]{2,1,0:T(8,128)(2,1)} %lat_h.1, ...), custom_call_target="tpu_custom_call" | custom-call | tf_op jit(solution)/shard_map/pallas_call | solution.py:304
  10.4 1.3 %collective-permute-start.8 = (bf16[256,1280]{1,0:T(8,128)(2,1)S(1)}, bf16[256,1280]{1,0:T(8,128)(2,1)S(1)}, u32[]{:S(2)}, u32[]{:S(2)}) collective-permute-start(bf16[256,1280]{1,0:T(8,128)(2,1)S(1)} %get-tuple-element.29), channel_id=1, source_target_pairs={{0,96},{1,97},{2,98},{3,99},{4,100},{5,101},{6,102},{7,103},{8,104... | collective-permute-start | bytes 1966088 | tf_op jit(solution)/shard_map/ppermute | solution.py:255
  13.3 1.6 %collective-permute-start.2 = (s32[2,32]{1,0:T(2,128)S(1)}, s32[2,32]{1,0:T(2,128)S(1)}, u32[]{:S(2)}, u32[]{:S(2)}) collective-permute-start(s32[2,32]{1,0:T(2,128)S(1)} %shard_map.93.refs_0_), channel_id=1, source_target_pairs={{0,1},{1,2},{2,3},{3,0},{4,5},{5,6},{6,7},{7,4},{8,9},{9,10},{10,1... | collective-permute-start | bytes 776 | tf_op jit(solution)/shard_map/ppermute | solution.py:281
  14.8 2.7 %collective-permute-start.3 = (s32[2,32]{1,0:T(2,128)S(1)}, s32[2,32]{1,0:T(2,128)S(1)}, u32[]{:S(2)}, u32[]{:S(2)}) collective-permute-start(s32[2,32]{1,0:T(2,128)S(1)} %shard_map.93.refs_0_), channel_id=1, source_target_pairs={{0,2},{1,3},{2,0},{3,1},{4,6},{5,7},{6,4},{7,5},{8,10},{9,11},{10,... | collective-permute-start | bytes 776 | tf_op jit(solution)/shard_map/ppermute | solution.py:281
  17.6 1.4 %collective-permute-start.4 = (s32[2,32]{1,0:T(2,128)S(1)}, s32[2,32]{1,0:T(2,128)S(1)}, u32[]{:S(2)}, u32[]{:S(2)}) collective-permute-start(s32[2,32]{1,0:T(2,128)S(1)} %shard_map.93.refs_0_), channel_id=1, source_target_pairs={{0,3},{1,0},{2,1},{3,2},{4,7},{5,4},{6,5},{7,6},{8,11},{9,8},{10,9... | collective-permute-start | bytes 776 | tf_op jit(solution)/shard_map/ppermute | solution.py:281
  19.0 0.9 %collective-permute-done.3.refs_2_ = s32[2,32]{1,0:T(2,128)S(1)} collective-permute-done((s32[2,32]{1,0:T(2,128)S(1)}, s32[2,32]{1,0:T(2,128)S(1)}, u32[]{:S(2)}, u32[]{:S(2)}) %collective-permute-start.3) | collective-permute-done | bytes 288 | tf_op jit(solution)/shard_map/ppermute | solution.py:281
  19.9 1.2 %collective-permute-done.4.refs_3_ = s32[2,32]{1,0:T(2,128)S(1)} collective-permute-done((s32[2,32]{1,0:T(2,128)S(1)}, s32[2,32]{1,0:T(2,128)S(1)}, u32[]{:S(2)}, u32[]{:S(2)}) %collective-permute-start.4) | collective-permute-done | bytes 288 | tf_op jit(solution)/shard_map/ppermute | solution.py:281
  21.1 1.6 %collective-permute-start.5 = (s32[2,32]{1,0:T(2,128)S(1)}, s32[2,32]{1,0:T(2,128)S(1)}, u32[]{:S(2)}, u32[]{:S(2)}) collective-permute-start(s32[2,32]{1,0:T(2,128)S(1)} %shard_map.95.refs_0_), channel_id=1, source_target_pairs={{0,4},{1,5},{2,6},{3,7},{4,8},{5,9},{6,10},{7,11},{8,12},{9,13},{1... | collective-permute-start | bytes 776 | tf_op jit(solution)/shard_map/ppermute | solution.py:281
  22.8 2.9 %collective-permute-start.6 = (s32[2,32]{1,0:T(2,128)S(1)}, s32[2,32]{1,0:T(2,128)S(1)}, u32[]{:S(2)}, u32[]{:S(2)}) collective-permute-start(s32[2,32]{1,0:T(2,128)S(1)} %shard_map.95.refs_0_), channel_id=1, source_target_pairs={{0,8},{1,9},{2,10},{3,11},{4,12},{5,13},{6,14},{7,15},{8,0},{9,1},... | collective-permute-start | bytes 776 | tf_op jit(solution)/shard_map/ppermute | solution.py:281
  25.7 1.3 %collective-permute-start.7 = (s32[2,32]{1,0:T(2,128)S(1)}, s32[2,32]{1,0:T(2,128)S(1)}, u32[]{:S(2)}, u32[]{:S(2)}) collective-permute-start(s32[2,32]{1,0:T(2,128)S(1)} %shard_map.95.refs_0_), channel_id=1, source_target_pairs={{0,12},{1,13},{2,14},{3,15},{4,0},{5,1},{6,2},{7,3},{8,4},{9,5},{1... | collective-permute-start | bytes 776 | tf_op jit(solution)/shard_map/ppermute | solution.py:281
  27.9 1.4 %collective-permute-done.7.refs_3_ = s32[2,32]{1,0:T(2,128)S(1)} collective-permute-done((s32[2,32]{1,0:T(2,128)S(1)}, s32[2,32]{1,0:T(2,128)S(1)}, u32[]{:S(2)}, u32[]{:S(2)}) %collective-permute-start.7) | collective-permute-done | bytes 288 | tf_op jit(solution)/shard_map/ppermute | solution.py:281
  29.3 2.5 %shard_map.97 = bf16[128,1280]{1,0:T(8,128)(2,1)S(1)} custom-call(f32[1,1280]{1,0:T(1,128)S(1)} %get-tuple-element.30.refs_0_, bf16[1280,2560]{1,0:T(8,128)(2,1)S(1)} %get-tuple-element.31.refs_1_, bf16[2560,1280]{1,0:T(8,128)(2,1)S(1)} %get-tuple-element.32.refs_2_, s32[2,32]{1,0:T(2,128)S(1)} %shard_map.96.refs_3_, ...), custom_call_target="tpu_custom_call" | custom-call | flops 13421772800 | bytes 1048576 | tf_op jit(solution)/shard_map/pallas_call | solution.py:363
  31.8 1.5 %collective-permute-start.10 = (bf16[128,1280]{1,0:T(8,128)(2,1)S(1)}, bf16[128,1280]{1,0:T(8,128)(2,1)S(1)}, u32[]{:S(2)}, u32[]{:S(2)}) collective-permute-start(bf16[128,1280]{1,0:T(8,128)(2,1)S(1)} %shard_map.97), channel_id=1, source_target_pairs={{0,32},{1,33},{2,34},{3,35},{4,36},{5,37},{6,38},{7,39},{8,40},{9,... | collective-permute-start | bytes 983048 | tf_op jit(solution)/shard_map/ppermute | solution.py:255
  33.3 1.3 %collective-permute-start.16 = (bf16[128,1280]{1,0:T(8,128)(2,1)S(1)}, bf16[128,1280]{1,0:T(8,128)(2,1)S(1)}, u32[]{:S(2)}, u32[]{:S(2)}) collective-permute-start(bf16[128,1280]{1,0:T(8,128)(2,1)S(1)} %shard_map.97), channel_id=1, source_target_pairs={{0,96},{1,97},{2,98},{3,99},{4,100},{5,101},{6,102},{7,103},{8,104... | collective-permute-start | bytes 983048 | tf_op jit(solution)/shard_map/ppermute | solution.py:255
  34.7 2.7 %shard_map.99.refs_4_ = bf16[128,1280]{1,0:T(8,128)(2,1)S(1)} custom-call(f32[1,1280]{1,0:T(1,128)S(1)} %get-tuple-element.30.refs_0_, bf16[1280,2560]{1,0:T(8,128)(2,1)S(1)} %get-tuple-element.31.refs_1_, bf16[2560,1280]{1,0:T(8,128)(2,1)S(1)} %get-tuple-element.32.refs_2_, s32[2,32]{1,0:T(2,128)S(1)} %shard_map.96.refs_3_, ...), custom_call_target="tpu_custom_call" | custom-call | flops 13421772800 | bytes 1048576 | tf_op jit(solution)/shard_map/pallas_call | solution.py:363
  38.7 1.3 %collective-permute-start.18 = (bf16[128,1280]{1,0:T(8,128)(2,1)S(1)}, bf16[128,1280]{1,0:T(8,128)(2,1)S(1)}, u32[]{:S(2)}, u32[]{:S(2)}) collective-permute-start(bf16[128,1280]{1,0:T(8,128)(2,1)S(1)} %shard_map.99.refs_4_), channel_id=1, source_target_pairs={{0,96},{1,97},{2,98},{3,99},{4,100},{5,101},{6,102},{7,103},{8,104... | collective-permute-start | bytes 983048 | tf_op jit(solution)/shard_map/ppermute | solution.py:255
  40.9 1.4 %collective-permute-done.14.refs_5_ = bf16[256,1280]{1,0:T(8,128)(2,1)S(1)} collective-permute-done((bf16[256,1280]{1,0:T(8,128)(2,1)S(1)}, bf16[256,1280]{1,0:T(8,128)(2,1)S(1)}, u32[]{:S(2)}, u32[]{:S(2)}) %collective-permute-start.14) | collective-permute-done | bytes 655392 | tf_op jit(solution)/shard_map/ppermute | solution.py:255
  42.3 2.3 %collective-permute-start.15 = (bf16[128,1280]{1,0:T(8,128)(2,1)S(1)}, bf16[128,1280]{1,0:T(8,128)(2,1)S(1)}, u32[]{:S(2)}, u32[]{:S(2)}) collective-permute-start(bf16[128,1280]{1,0:T(8,128)(2,1)S(1)} %shard_map.103.refs_4_), channel_id=1, source_target_pairs={{0,32},{1,33},{2,34},{3,35},{4,36},{5,37},{6,38},{7,39},{8,40},{9,... | collective-permute-start | bytes 983048 | tf_op jit(solution)/shard_map/ppermute | solution.py:255
  44.6 1.2 %collective-permute-done.15.refs_6_ = bf16[128,1280]{1,0:T(8,128)(2,1)S(1)} collective-permute-done((bf16[128,1280]{1,0:T(8,128)(2,1)S(1)}, bf16[128,1280]{1,0:T(8,128)(2,1)S(1)}, u32[]{:S(2)}, u32[]{:S(2)}) %collective-permute-start.15) | collective-permute-done | bytes 327712 | tf_op jit(solution)/shard_map/ppermute | solution.py:255
  45.9 4.0 %collective-permute-start.17 = (bf16[128,1280]{1,0:T(8,128)(2,1)S(1)}, bf16[128,1280]{1,0:T(8,128)(2,1)S(1)}, u32[]{:S(2)}, u32[]{:S(2)}) collective-permute-start(bf16[128,1280]{1,0:T(8,128)(2,1)S(1)} %shard_map.104), channel_id=1, source_target_pairs={{0,32},{1,33},{2,34},{3,35},{4,36},{5,37},{6,38},{7,39},{8,40},{9,... | collective-permute-start | bytes 983048 | tf_op jit(solution)/shard_map/ppermute | solution.py:255
  49.9 1.3 %collective-permute-done.17.refs_6_ = bf16[128,1280]{1,0:T(8,128)(2,1)S(1)} collective-permute-done((bf16[128,1280]{1,0:T(8,128)(2,1)S(1)}, bf16[128,1280]{1,0:T(8,128)(2,1)S(1)}, u32[]{:S(2)}, u32[]{:S(2)}) %collective-permute-start.17) | collective-permute-done | bytes 327712 | tf_op jit(solution)/shard_map/ppermute | solution.py:255
  52.5 1.3 %collective-permute-start.21 = (bf16[6,8,256]{2,1,0:T(8,128)(2,1)S(1)}, bf16[6,8,256]{2,1,0:T(8,128)(2,1)S(1)}, u32[]{:S(2)}, u32[]{:S(2)}) collective-permute-start(bf16[6,8,256]{2,1,0:T(8,128)(2,1)S(1)} %get-tuple-element.43), channel_id=1, source_target_pairs={{96,0},{97,1},{98,2},{99,3},{100,4},{101,5},{102,6},{103,7},{104,8... | collective-permute-start | bytes 73736 | tf_op jit(solution)/shard_map/ppermute | solution.py:255
  53.8 12.5 %collective-permute-done.21 = bf16[6,8,256]{2,1,0:T(8,128)(2,1)S(1)} collective-permute-done((bf16[6,8,256]{2,1,0:T(8,128)(2,1)S(1)}, bf16[6,8,256]{2,1,0:T(8,128)(2,1)S(1)}, u32[]{:S(2)}, u32[]{:S(2)}) %collective-permute-start.21) | collective-permute-done | bytes 24608 | tf_op jit(solution)/shard_map/ppermute | solution.py:255
  (39 shorter events, 7.3 us)
Async XLA Ops:
  0.0 0.7 %copy-start = (s32[2,2]{1,0:T(2,128)S(1)}, s32[2,2]{1,0:T(2,128)}, u32[]{:S(2)}) copy-start(s32[2,2]{1,0:T(2,128)} %anchors.1) | copy-start | bytes 52
  0.8 9.5 %collective-permute-start = (s32[2,32]{1,0:T(2,128)S(1)}, s32[2,32]{1,0:T(2,128)S(1)}, u32[]{:S(2)}, u32[]{:S(2)}) collective-permute-start(s32[2,32]{1,0:T(2,128)S(1)} %shard_map.92.refs_0_), channel_id=1, source_target_pairs={{0,16},{1,17},{2,18},{3,19},{4,20},{5,21},{6,22},{7,23},{8,24},{9,... | collective-permute-start | bytes 776 | tf_op jit(solution)/shard_map/ppermute | solution.py:281
  10.3 2.2 %collective-permute-start.1 = (bf16[256,1280]{1,0:T(8,128)(2,1)S(1)}, bf16[256,1280]{1,0:T(8,128)(2,1)S(1)}, u32[]{:S(2)}, u32[]{:S(2)}) collective-permute-start(bf16[256,1280]{1,0:T(8,128)(2,1)S(1)} %get-tuple-element.29), channel_id=1, source_target_pairs={{0,32},{1,33},{2,34},{3,35},{4,36},{5,37},{6,38},{7,39},{8,40},{9,... | collective-permute-start | bytes 1966088 | tf_op jit(solution)/shard_map/ppermute | solution.py:255
  10.4 18.8 %collective-permute-start.8 = (bf16[256,1280]{1,0:T(8,128)(2,1)S(1)}, bf16[256,1280]{1,0:T(8,128)(2,1)S(1)}, u32[]{:S(2)}, u32[]{:S(2)}) collective-permute-start(bf16[256,1280]{1,0:T(8,128)(2,1)S(1)} %get-tuple-element.29), channel_id=1, source_target_pairs={{0,96},{1,97},{2,98},{3,99},{4,100},{5,101},{6,102},{7,103},{8,104... | collective-permute-start | bytes 1966088 | tf_op jit(solution)/shard_map/ppermute | solution.py:255
  12.6 16.7 %collective-permute-start.9 = (bf16[256,1280]{1,0:T(8,128)(2,1)S(1)}, bf16[256,1280]{1,0:T(8,128)(2,1)S(1)}, u32[]{:S(2)}, u32[]{:S(2)}) collective-permute-start(bf16[256,1280]{1,0:T(8,128)(2,1)S(1)} %get-tuple-element.33), channel_id=1, source_target_pairs={{32,64},{33,65},{34,66},{35,67},{36,68},{37,69},{38,70},{39,71},{4... | collective-permute-start | bytes 1966088 | tf_op jit(solution)/shard_map/ppermute | solution.py:255
  13.3 5.7 %collective-permute-start.2 = (s32[2,32]{1,0:T(2,128)S(1)}, s32[2,32]{1,0:T(2,128)S(1)}, u32[]{:S(2)}, u32[]{:S(2)}) collective-permute-start(s32[2,32]{1,0:T(2,128)S(1)} %shard_map.93.refs_0_), channel_id=1, source_target_pairs={{0,1},{1,2},{2,3},{3,0},{4,5},{5,6},{6,7},{7,4},{8,9},{9,10},{10,1... | collective-permute-start | bytes 776 | tf_op jit(solution)/shard_map/ppermute | solution.py:281
  14.8 5.1 %collective-permute-start.3 = (s32[2,32]{1,0:T(2,128)S(1)}, s32[2,32]{1,0:T(2,128)S(1)}, u32[]{:S(2)}, u32[]{:S(2)}) collective-permute-start(s32[2,32]{1,0:T(2,128)S(1)} %shard_map.93.refs_0_), channel_id=1, source_target_pairs={{0,2},{1,3},{2,0},{3,1},{4,6},{5,7},{6,4},{7,5},{8,10},{9,11},{10,... | collective-permute-start | bytes 776 | tf_op jit(solution)/shard_map/ppermute | solution.py:281
  17.6 3.6 %collective-permute-start.4 = (s32[2,32]{1,0:T(2,128)S(1)}, s32[2,32]{1,0:T(2,128)S(1)}, u32[]{:S(2)}, u32[]{:S(2)}) collective-permute-start(s32[2,32]{1,0:T(2,128)S(1)} %shard_map.93.refs_0_), channel_id=1, source_target_pairs={{0,3},{1,0},{2,1},{3,2},{4,7},{5,4},{6,5},{7,6},{8,11},{9,8},{10,9... | collective-permute-start | bytes 776 | tf_op jit(solution)/shard_map/ppermute | solution.py:281
  21.1 5.9 %collective-permute-start.5 = (s32[2,32]{1,0:T(2,128)S(1)}, s32[2,32]{1,0:T(2,128)S(1)}, u32[]{:S(2)}, u32[]{:S(2)}) collective-permute-start(s32[2,32]{1,0:T(2,128)S(1)} %shard_map.95.refs_0_), channel_id=1, source_target_pairs={{0,4},{1,5},{2,6},{3,7},{4,8},{5,9},{6,10},{7,11},{8,12},{9,13},{1... | collective-permute-start | bytes 776 | tf_op jit(solution)/shard_map/ppermute | solution.py:281
  22.8 5.1 %collective-permute-start.6 = (s32[2,32]{1,0:T(2,128)S(1)}, s32[2,32]{1,0:T(2,128)S(1)}, u32[]{:S(2)}, u32[]{:S(2)}) collective-permute-start(s32[2,32]{1,0:T(2,128)S(1)} %shard_map.95.refs_0_), channel_id=1, source_target_pairs={{0,8},{1,9},{2,10},{3,11},{4,12},{5,13},{6,14},{7,15},{8,0},{9,1},... | collective-permute-start | bytes 776 | tf_op jit(solution)/shard_map/ppermute | solution.py:281
  25.7 3.6 %collective-permute-start.7 = (s32[2,32]{1,0:T(2,128)S(1)}, s32[2,32]{1,0:T(2,128)S(1)}, u32[]{:S(2)}, u32[]{:S(2)}) collective-permute-start(s32[2,32]{1,0:T(2,128)S(1)} %shard_map.95.refs_0_), channel_id=1, source_target_pairs={{0,12},{1,13},{2,14},{3,15},{4,0},{5,1},{6,2},{7,3},{8,4},{9,5},{1... | collective-permute-start | bytes 776 | tf_op jit(solution)/shard_map/ppermute | solution.py:281
  31.8 2.8 %collective-permute-start.10 = (bf16[128,1280]{1,0:T(8,128)(2,1)S(1)}, bf16[128,1280]{1,0:T(8,128)(2,1)S(1)}, u32[]{:S(2)}, u32[]{:S(2)}) collective-permute-start(bf16[128,1280]{1,0:T(8,128)(2,1)S(1)} %shard_map.97), channel_id=1, source_target_pairs={{0,32},{1,33},{2,34},{3,35},{4,36},{5,37},{6,38},{7,39},{8,40},{9,... | collective-permute-start | bytes 983048 | tf_op jit(solution)/shard_map/ppermute | solution.py:255
  33.3 11.3 %collective-permute-start.16 = (bf16[128,1280]{1,0:T(8,128)(2,1)S(1)}, bf16[128,1280]{1,0:T(8,128)(2,1)S(1)}, u32[]{:S(2)}, u32[]{:S(2)}) collective-permute-start(bf16[128,1280]{1,0:T(8,128)(2,1)S(1)} %shard_map.97), channel_id=1, source_target_pairs={{0,96},{1,97},{2,98},{3,99},{4,100},{5,101},{6,102},{7,103},{8,104... | collective-permute-start | bytes 983048 | tf_op jit(solution)/shard_map/ppermute | solution.py:255
  37.4 4.9 %collective-permute-start.13 = (bf16[128,1280]{1,0:T(8,128)(2,1)S(1)}, bf16[128,1280]{1,0:T(8,128)(2,1)S(1)}, u32[]{:S(2)}, u32[]{:S(2)}) collective-permute-start(bf16[128,1280]{1,0:T(8,128)(2,1)S(1)} %shard_map.98.refs_7_), channel_id=1, source_target_pairs={{32,64},{33,65},{34,66},{35,67},{36,68},{37,69},{38,70},{39,71},{4... | collective-permute-start | bytes 983048 | tf_op jit(solution)/shard_map/ppermute | solution.py:255
  38.1 2.1 %collective-permute-start.11 = (bf16[128,1280]{1,0:T(8,128)(2,1)S(1)}, bf16[128,1280]{1,0:T(8,128)(2,1)S(1)}, u32[]{:S(2)}, u32[]{:S(2)}) collective-permute-start(bf16[128,1280]{1,0:T(8,128)(2,1)S(1)} %shard_map.99.refs_4_), channel_id=1, source_target_pairs={{0,32},{1,33},{2,34},{3,35},{4,36},{5,37},{6,38},{7,39},{8,40},{9,... | collective-permute-start | bytes 983048 | tf_op jit(solution)/shard_map/ppermute | solution.py:255
  38.7 11.2 %collective-permute-start.18 = (bf16[128,1280]{1,0:T(8,128)(2,1)S(1)}, bf16[128,1280]{1,0:T(8,128)(2,1)S(1)}, u32[]{:S(2)}, u32[]{:S(2)}) collective-permute-start(bf16[128,1280]{1,0:T(8,128)(2,1)S(1)} %shard_map.99.refs_4_), channel_id=1, source_target_pairs={{0,96},{1,97},{2,98},{3,99},{4,100},{5,101},{6,102},{7,103},{8,104... | collective-permute-start | bytes 983048 | tf_op jit(solution)/shard_map/ppermute | solution.py:255
  40.1 2.2 %collective-permute-start.14 = (bf16[256,1280]{1,0:T(8,128)(2,1)S(1)}, bf16[256,1280]{1,0:T(8,128)(2,1)S(1)}, u32[]{:S(2)}, u32[]{:S(2)}) collective-permute-start(bf16[256,1280]{1,0:T(8,128)(2,1)S(1)} %shard_map.100.refs_4_), channel_id=1, source_target_pairs={{0,32},{1,33},{2,34},{3,35},{4,36},{5,37},{6,38},{7,39},{8,40},{9,... | collective-permute-start | bytes 1966088 | tf_op jit(solution)/shard_map/ppermute | solution.py:255
  40.2 4.4 %collective-permute-start.12 = (bf16[128,1280]{1,0:T(8,128)(2,1)S(1)}, bf16[128,1280]{1,0:T(8,128)(2,1)S(1)}, u32[]{:S(2)}, u32[]{:S(2)}) collective-permute-start(bf16[128,1280]{1,0:T(8,128)(2,1)S(1)} %shard_map.101.refs_7_), channel_id=1, source_target_pairs={{32,64},{33,65},{34,66},{35,67},{36,68},{37,69},{38,70},{39,71},{4... | collective-permute-start | bytes 983048 | tf_op jit(solution)/shard_map/ppermute | solution.py:255
  42.3 3.6 %collective-permute-start.15 = (bf16[128,1280]{1,0:T(8,128)(2,1)S(1)}, bf16[128,1280]{1,0:T(8,128)(2,1)S(1)}, u32[]{:S(2)}, u32[]{:S(2)}) collective-permute-start(bf16[128,1280]{1,0:T(8,128)(2,1)S(1)} %shard_map.103.refs_4_), channel_id=1, source_target_pairs={{0,32},{1,33},{2,34},{3,35},{4,36},{5,37},{6,38},{7,39},{8,40},{9,... | collective-permute-start | bytes 983048 | tf_op jit(solution)/shard_map/ppermute | solution.py:255
  45.9 5.3 %collective-permute-start.17 = (bf16[128,1280]{1,0:T(8,128)(2,1)S(1)}, bf16[128,1280]{1,0:T(8,128)(2,1)S(1)}, u32[]{:S(2)}, u32[]{:S(2)}) collective-permute-start(bf16[128,1280]{1,0:T(8,128)(2,1)S(1)} %shard_map.104), channel_id=1, source_target_pairs={{0,32},{1,33},{2,34},{3,35},{4,36},{5,37},{6,38},{7,39},{8,40},{9,... | collective-permute-start | bytes 983048 | tf_op jit(solution)/shard_map/ppermute | solution.py:255
  51.2 2.6 %collective-permute-start.19 = (bf16[6,8,256]{2,1,0:T(8,128)(2,1)S(1)}, bf16[6,8,256]{2,1,0:T(8,128)(2,1)S(1)}, u32[]{:S(2)}, u32[]{:S(2)}) collective-permute-start(bf16[6,8,256]{2,1,0:T(8,128)(2,1)S(1)} %get-tuple-element.41), channel_id=1, source_target_pairs={{96,64},{97,65},{98,66},{99,67},{100,68},{101,69},{102,70},{103,71... | collective-permute-start | bytes 73736 | tf_op jit(solution)/shard_map/ppermute | solution.py:255
  51.8 2.0 %collective-permute-start.20 = (bf16[6,8,256]{2,1,0:T(8,128)(2,1)S(1)}, bf16[6,8,256]{2,1,0:T(8,128)(2,1)S(1)}, u32[]{:S(2)}, u32[]{:S(2)}) collective-permute-start(bf16[6,8,256]{2,1,0:T(8,128)(2,1)S(1)} %get-tuple-element.42), channel_id=1, source_target_pairs={{96,32},{97,33},{98,34},{99,35},{100,36},{101,37},{102,38},{103,39... | collective-permute-start | bytes 73736 | tf_op jit(solution)/shard_map/ppermute | solution.py:255
  52.5 13.8 %collective-permute-start.21 = (bf16[6,8,256]{2,1,0:T(8,128)(2,1)S(1)}, bf16[6,8,256]{2,1,0:T(8,128)(2,1)S(1)}, u32[]{:S(2)}, u32[]{:S(2)}) collective-permute-start(bf16[6,8,256]{2,1,0:T(8,128)(2,1)S(1)} %get-tuple-element.43), channel_id=1, source_target_pairs={{96,0},{97,1},{98,2},{99,3},{100,4},{101,5},{102,6},{103,7},{104,8... | collective-permute-start | bytes 73736 | tf_op jit(solution)/shard_map/ppermute | solution.py:255

commit v2 on v1

--- a/solution.py
+++ b/solution.py
@@ -405,9 +405,9 @@
     t3, _ = lax.optimization_barrier((t3, d2))
     third3 = swap(t3)
     bands = tick({3: (3,)}, {}, near3=third3, first3=first3, sums=d2)
-    sent = [hop(a, (3, s)) for s, a in enumerate(bands[f"band{k}"] for k in range(3))]
+    sent = {s: hop(bands[f"band{s}"], (3, s)) for s in (0, 1, 2)}
     result = bands["band3"]
-    for s in range(3):
+    for s in (2, 1, 0):
         result = jnp.where(section == s, sent[s], result)
     return result
 

time: 67.2 us -> 66.7 us (level)
  the two profiles are of different devices: /device:TPU:0 before, /device:TPU:1 now
where the time goes in v2:
time: 66.7 us; the launch traced here: 66.4 us
  starting transfers between devices  27.3 us (41%)
  waiting for transfers between devices  22.7 us (34%)
  Pallas kernels  14.8 us (22%)
  local copies, waits for them, and re-layouts  0.68 us (1%)
    ppermute x15, waiting for transfers between devices, hop(): lax.ppermute(value, axes, [(a * slabs + w, b * slabs + w) for a, b in pai...  20.1 us
    ppermute x15, starting transfers between devices, hop(): lax.ppermute(value, axes, [(a * slabs + w, b * slabs + w) for a, b in pai...  14.6 us
    ppermute x7, starting transfers between devices, join(): others = [lax.ppermute(tables[-1], 'win', p) for p in pairs]  12.6 us
    pallas_call x11, Pallas kernels, tick(): pl.pallas_call(functools.partial(tick_kernel, roles, outs, [*given, *made...  9.34 us
    pallas_call x1, Pallas kernels, per_device(): pl.pallas_call(functools.partial(load_kernel, chunks), out_shape=[act(2),...  5.37 us
    ppermute x7, waiting for transfers between devices, join(): others = [lax.ppermute(tables[-1], 'win', p) for p in pairs]  2.62 us
  transfers between devices with their start and end apart: 22, of which 10 were waited for; matrix products, arithmetic and copies ran while one was open for 0% of the time, Pallas kernels for 22%

profile of v2, /device:TPU:1, one launch (start us, length us, event | category | flops | bytes accessed | tf_op | source)
XLA Modules:
  0.0 66.4 jit_solution(11509029915729466426)
XLA Ops:
  0.8 2.5 %collective-permute-start = (s32[2,32]{1,0:T(2,128)S(1)}, s32[2,32]{1,0:T(2,128)S(1)}, u32[]{:S(2)}, u32[]{:S(2)}) collective-permute-start(s32[2,32]{1,0:T(2,128)S(1)} %shard_map.92.refs_0_), channel_id=1, source_target_pairs={{0,16},{1,17},{2,18},{3,19},{4,20},{5,21},{6,22},{7,23},{8,24},{9,... | collective-permute-start | bytes 776 | tf_op jit(solution)/shard_map/ppermute | solution.py:281
  3.3 5.4 %shard_map.91 = (bf16[256,1280]{1,0:T(8,128)(2,1)S(1)}, bf16[24,8,256]{2,1,0:T(8,128)(2,1)S(1)}, bf16[256,1280]{1,0:T(8,128)(2,1)S(1)}, bf16[16,2,8,1280]{3,2,1,...) custom-call(bf16[24,8,256]{2,1,0:T(8,128)(2,1)} %lat_h.1, ...), custom_call_target="tpu_custom_call" | custom-call | tf_op jit(solution)/shard_map/pallas_call | solution.py:304
  8.7 3.1 %collective-permute-start.1 = (bf16[256,1280]{1,0:T(8,128)(2,1)S(1)}, bf16[256,1280]{1,0:T(8,128)(2,1)S(1)}, u32[]{:S(2)}, u32[]{:S(2)}) collective-permute-start(bf16[256,1280]{1,0:T(8,128)(2,1)S(1)} %get-tuple-element.29), channel_id=1, source_target_pairs={{0,32},{1,33},{2,34},{3,35},{4,36},{5,37},{6,38},{7,39},{8,40},{9,... | collective-permute-start | bytes 1966088 | tf_op jit(solution)/shard_map/ppermute | solution.py:255
  12.5 1.0 %collective-permute-done.1.refs_3_ = bf16[256,1280]{1,0:T(8,128)(2,1)S(1)} collective-permute-done((bf16[256,1280]{1,0:T(8,128)(2,1)S(1)}, bf16[256,1280]{1,0:T(8,128)(2,1)S(1)}, u32[]{:S(2)}, u32[]{:S(2)}) %collective-permute-start.1) | collective-permute-done | bytes 655392 | tf_op jit(solution)/shard_map/ppermute | solution.py:255
  13.5 4.6 %shard_map.94 = (bf16[256,1280]{1,0:T(8,128)(2,1)S(1)}, f32[1,1280]{1,0:T(1,128)S(1)}, bf16[1280,2560]{1,0:T(8,128)(2,1)S(1)}, bf16[2560,1280]{1,0:T(8,128)(2,1)...) custom-call(f32[1,1280]{1,0:T(1,128)S(1)} %get-tuple-element.25.refs, ...), custom_call_target="tpu_custom_call", output_to_operand_aliasing={{1}: (0, {}), {2}: (1, {}), {3}: (2, {})} | custom-call | flops 26843545600 | bytes 1048576 | tf_op jit(solution)/shard_map/pallas_call | solution.py:363
  18.2 1.3 %collective-permute-start.9 = (bf16[256,1280]{1,0:T(8,128)(2,1)S(1)}, bf16[256,1280]{1,0:T(8,128)(2,1)S(1)}, u32[]{:S(2)}, u32[]{:S(2)}) collective-permute-start(bf16[256,1280]{1,0:T(8,128)(2,1)S(1)} %get-tuple-element.33), channel_id=1, source_target_pairs={{32,64},{33,65},{34,66},{35,67},{36,68},{37,69},{38,70},{39,71},{4... | collective-permute-start | bytes 1966088 | tf_op jit(solution)/shard_map/ppermute | solution.py:255
  19.5 1.3 %collective-permute-start.2 = (s32[2,32]{1,0:T(2,128)S(1)}, s32[2,32]{1,0:T(2,128)S(1)}, u32[]{:S(2)}, u32[]{:S(2)}) collective-permute-start(s32[2,32]{1,0:T(2,128)S(1)} %shard_map.93.refs_0_), channel_id=1, source_target_pairs={{0,1},{1,2},{2,3},{3,0},{4,5},{5,6},{6,7},{7,4},{8,9},{9,10},{10,1... | collective-permute-start | bytes 776 | tf_op jit(solution)/shard_map/ppermute | solution.py:281
  20.8 2.5 %collective-permute-start.3 = (s32[2,32]{1,0:T(2,128)S(1)}, s32[2,32]{1,0:T(2,128)S(1)}, u32[]{:S(2)}, u32[]{:S(2)}) collective-permute-start(s32[2,32]{1,0:T(2,128)S(1)} %shard_map.93.refs_0_), channel_id=1, source_target_pairs={{0,2},{1,3},{2,0},{3,1},{4,6},{5,7},{6,4},{7,5},{8,10},{9,11},{10,... | collective-permute-start | bytes 776 | tf_op jit(solution)/shard_map/ppermute | solution.py:281
  23.2 1.1 %collective-permute-start.4 = (s32[2,32]{1,0:T(2,128)S(1)}, s32[2,32]{1,0:T(2,128)S(1)}, u32[]{:S(2)}, u32[]{:S(2)}) collective-permute-start(s32[2,32]{1,0:T(2,128)S(1)} %shard_map.93.refs_0_), channel_id=1, source_target_pairs={{0,3},{1,0},{2,1},{3,2},{4,7},{5,4},{6,5},{7,6},{8,11},{9,8},{10,9... | collective-permute-start | bytes 776 | tf_op jit(solution)/shard_map/ppermute | solution.py:281
  25.7 1.5 %collective-permute-start.5 = (s32[2,32]{1,0:T(2,128)S(1)}, s32[2,32]{1,0:T(2,128)S(1)}, u32[]{:S(2)}, u32[]{:S(2)}) collective-permute-start(s32[2,32]{1,0:T(2,128)S(1)} %shard_map.95.refs_0_), channel_id=1, source_target_pairs={{0,4},{1,5},{2,6},{3,7},{4,8},{5,9},{6,10},{7,11},{8,12},{9,13},{1... | collective-permute-start | bytes 776 | tf_op jit(solution)/shard_map/ppermute | solution.py:281
  27.2 2.6 %collective-permute-start.6 = (s32[2,32]{1,0:T(2,128)S(1)}, s32[2,32]{1,0:T(2,128)S(1)}, u32[]{:S(2)}, u32[]{:S(2)}) collective-permute-start(s32[2,32]{1,0:T(2,128)S(1)} %shard_map.95.refs_0_), channel_id=1, source_target_pairs={{0,8},{1,9},{2,10},{3,11},{4,12},{5,13},{6,14},{7,15},{8,0},{9,1},... | collective-permute-start | bytes 776 | tf_op jit(solution)/shard_map/ppermute | solution.py:281
  29.8 1.1 %collective-permute-start.7 = (s32[2,32]{1,0:T(2,128)S(1)}, s32[2,32]{1,0:T(2,128)S(1)}, u32[]{:S(2)}, u32[]{:S(2)}) collective-permute-start(s32[2,32]{1,0:T(2,128)S(1)} %shard_map.95.refs_0_), channel_id=1, source_target_pairs={{0,12},{1,13},{2,14},{3,15},{4,0},{5,1},{6,2},{7,3},{8,4},{9,5},{1... | collective-permute-start | bytes 776 | tf_op jit(solution)/shard_map/ppermute | solution.py:281
  31.1 1.1 %collective-permute-done.7.refs_3_ = s32[2,32]{1,0:T(2,128)S(1)} collective-permute-done((s32[2,32]{1,0:T(2,128)S(1)}, s32[2,32]{1,0:T(2,128)S(1)}, u32[]{:S(2)}, u32[]{:S(2)}) %collective-permute-start.7) | collective-permute-done | bytes 288 | tf_op jit(solution)/shard_map/ppermute | solution.py:281
  32.3 1.3 %collective-permute-start.10 = (bf16[128,1280]{1,0:T(8,128)(2,1)S(1)}, bf16[128,1280]{1,0:T(8,128)(2,1)S(1)}, u32[]{:S(2)}, u32[]{:S(2)}) collective-permute-start(bf16[128,1280]{1,0:T(8,128)(2,1)S(1)} %shard_map.97), channel_id=1, source_target_pairs={{0,32},{1,33},{2,34},{3,35},{4,36},{5,37},{6,38},{7,39},{8,40},{9,... | collective-permute-start | bytes 983048 | tf_op jit(solution)/shard_map/ppermute | solution.py:255
  34.3 1.5 %collective-permute-done.10.refs_3_ = bf16[128,1280]{1,0:T(8,128)(2,1)S(1)} collective-permute-done((bf16[128,1280]{1,0:T(8,128)(2,1)S(1)}, bf16[128,1280]{1,0:T(8,128)(2,1)S(1)}, u32[]{:S(2)}, u32[]{:S(2)}) %collective-permute-start.10) | collective-permute-done | bytes 327712 | tf_op jit(solution)/shard_map/ppermute | solution.py:255
  35.8 2.2 %shard_map.98.refs_7_ = bf16[128,1280]{1,0:T(8,128)(2,1)S(1)} custom-call(f32[1,1280]{1,0:T(1,128)S(1)} %get-tuple-element.30.refs_0_, bf16[1280,2560]{1,0:T(8,128)(2,1)S(1)} %get-tuple-element.31.refs_1_, bf16[2560,1280]{1,0:T(8,128)(2,1)S(1)} %get-tuple-element.32.refs_2_, bf16[128,1280]{1,0:T(8,128)(2,1)S(1)} %collective-permute-done.10.refs_3_), custom_call_target="tpu_custom_call" | custom-call | flops 13421772800 | bytes 1048576 | tf_op jit(solution)/shard_map/pallas_call | solution.py:363
  38.3 1.3 %collective-permute-start.13 = (bf16[128,1280]{1,0:T(8,128)(2,1)S(1)}, bf16[128,1280]{1,0:T(8,128)(2,1)S(1)}, u32[]{:S(2)}, u32[]{:S(2)}) collective-permute-start(bf16[128,1280]{1,0:T(8,128)(2,1)S(1)} %shard_map.98.refs_7_), channel_id=1, source_target_pairs={{32,64},{33,65},{34,66},{35,67},{36,68},{37,69},{38,70},{39,71},{4... | collective-permute-start | bytes 983048 | tf_op jit(solution)/shard_map/ppermute | solution.py:255
  40.4 1.2 %collective-permute-start.14 = (bf16[256,1280]{1,0:T(8,128)(2,1)S(1)}, bf16[256,1280]{1,0:T(8,128)(2,1)S(1)}, u32[]{:S(2)}, u32[]{:S(2)}) collective-permute-start(bf16[256,1280]{1,0:T(8,128)(2,1)S(1)} %shard_map.100.refs_4_), channel_id=1, source_target_pairs={{0,32},{1,33},{2,34},{3,35},{4,36},{5,37},{6,38},{7,39},{8,40},{9,... | collective-permute-start | bytes 1966088 | tf_op jit(solution)/shard_map/ppermute | solution.py:255
  41.6 2.2 %shard_map.101.refs_7_ = bf16[128,1280]{1,0:T(8,128)(2,1)S(1)} custom-call(f32[1,1280]{1,0:T(1,128)S(1)} %get-tuple-element.30.refs_0_, bf16[1280,2560]{1,0:T(8,128)(2,1)S(1)} %get-tuple-element.31.refs_1_, bf16[2560,1280]{1,0:T(8,128)(2,1)S(1)} %get-tuple-element.32.refs_2_, bf16[128,1280]{1,0:T(8,128)(2,1)S(1)} %collective-permute-done.11.refs_3_, ...), custom_call_target="tpu_custom_call" | custom-call | flops 13421772800 | bytes 1048576 | tf_op jit(solution)/shard_map/pallas_call | solution.py:363
  43.8 1.3 %collective-permute-start.12 = (bf16[128,1280]{1,0:T(8,128)(2,1)S(1)}, bf16[128,1280]{1,0:T(8,128)(2,1)S(1)}, u32[]{:S(2)}, u32[]{:S(2)}) collective-permute-start(bf16[128,1280]{1,0:T(8,128)(2,1)S(1)} %shard_map.101.refs_7_), channel_id=1, source_target_pairs={{32,64},{33,65},{34,66},{35,67},{36,68},{37,69},{38,70},{39,71},{4... | collective-permute-start | bytes 983048 | tf_op jit(solution)/shard_map/ppermute | solution.py:255
  45.5 5.2 %collective-permute-done.12.refs_3_ = bf16[128,1280]{1,0:T(8,128)(2,1)S(1)} collective-permute-done((bf16[128,1280]{1,0:T(8,128)(2,1)S(1)}, bf16[128,1280]{1,0:T(8,128)(2,1)S(1)}, u32[]{:S(2)}, u32[]{:S(2)}) %collective-permute-start.12) | collective-permute-done | bytes 327712 | tf_op jit(solution)/shard_map/ppermute | solution.py:255
  50.8 1.6 %collective-permute-done.17.refs_6_ = bf16[128,1280]{1,0:T(8,128)(2,1)S(1)} collective-permute-done((bf16[128,1280]{1,0:T(8,128)(2,1)S(1)}, bf16[128,1280]{1,0:T(8,128)(2,1)S(1)}, u32[]{:S(2)}, u32[]{:S(2)}) %collective-permute-start.17) | collective-permute-done | bytes 327712 | tf_op jit(solution)/shard_map/ppermute | solution.py:255
  53.1 1.3 %collective-permute-start.20 = (bf16[6,8,256]{2,1,0:T(8,128)(2,1)S(1)}, bf16[6,8,256]{2,1,0:T(8,128)(2,1)S(1)}, u32[]{:S(2)}, u32[]{:S(2)}) collective-permute-start(bf16[6,8,256]{2,1,0:T(8,128)(2,1)S(1)} %get-tuple-element.42), channel_id=1, source_target_pairs={{96,32},{97,33},{98,34},{99,35},{100,36},{101,37},{102,38},{103,39... | collective-permute-start | bytes 73736 | tf_op jit(solution)/shard_map/ppermute | solution.py:255
  55.1 10.7 %collective-permute-done.20 = bf16[6,8,256]{2,1,0:T(8,128)(2,1)S(1)} collective-permute-done((bf16[6,8,256]{2,1,0:T(8,128)(2,1)S(1)}, bf16[6,8,256]{2,1,0:T(8,128)(2,1)S(1)}, u32[]{:S(2)}, u32[]{:S(2)}) %collective-permute-start.20) | collective-permute-done | bytes 24608 | tf_op jit(solution)/shard_map/ppermute | solution.py:255
  (39 shorter events, 7.1 us)
Async XLA Ops:
  0.0 0.7 %copy-start = (s32[2,2]{1,0:T(2,128)S(1)}, s32[2,2]{1,0:T(2,128)}, u32[]{:S(2)}) copy-start(s32[2,2]{1,0:T(2,128)} %anchors.1) | copy-start | bytes 52
  0.8 7.9 %collective-permute-start = (s32[2,32]{1,0:T(2,128)S(1)}, s32[2,32]{1,0:T(2,128)S(1)}, u32[]{:S(2)}, u32[]{:S(2)}) collective-permute-start(s32[2,32]{1,0:T(2,128)S(1)} %shard_map.92.refs_0_), channel_id=1, source_target_pairs={{0,16},{1,17},{2,18},{3,19},{4,20},{5,21},{6,22},{7,23},{8,24},{9,... | collective-permute-start | bytes 776 | tf_op jit(solution)/shard_map/ppermute | solution.py:281
  8.7 4.8 %collective-permute-start.1 = (bf16[256,1280]{1,0:T(8,128)(2,1)S(1)}, bf16[256,1280]{1,0:T(8,128)(2,1)S(1)}, u32[]{:S(2)}, u32[]{:S(2)}) collective-permute-start(bf16[256,1280]{1,0:T(8,128)(2,1)S(1)} %get-tuple-element.29), channel_id=1, source_target_pairs={{0,32},{1,33},{2,34},{3,35},{4,36},{5,37},{6,38},{7,39},{8,40},{9,... | collective-permute-start | bytes 1966088 | tf_op jit(solution)/shard_map/ppermute | solution.py:255
  11.8 20.4 %collective-permute-start.8 = (bf16[256,1280]{1,0:T(8,128)(2,1)S(1)}, bf16[256,1280]{1,0:T(8,128)(2,1)S(1)}, u32[]{:S(2)}, u32[]{:S(2)}) collective-permute-start(bf16[256,1280]{1,0:T(8,128)(2,1)S(1)} %get-tuple-element.29), channel_id=1, source_target_pairs={{0,96},{1,97},{2,98},{3,99},{4,100},{5,101},{6,102},{7,103},{8,104... | collective-permute-start | bytes 1966088 | tf_op jit(solution)/shard_map/ppermute | solution.py:255
  18.2 14.1 %collective-permute-start.9 = (bf16[256,1280]{1,0:T(8,128)(2,1)S(1)}, bf16[256,1280]{1,0:T(8,128)(2,1)S(1)}, u32[]{:S(2)}, u32[]{:S(2)}) collective-permute-start(bf16[256,1280]{1,0:T(8,128)(2,1)S(1)} %get-tuple-element.33), channel_id=1, source_target_pairs={{32,64},{33,65},{34,66},{35,67},{36,68},{37,69},{38,70},{39,71},{4... | collective-permute-start | bytes 1966088 | tf_op jit(solution)/shard_map/ppermute | solution.py:255
  19.5 4.9 %collective-permute-start.2 = (s32[2,32]{1,0:T(2,128)S(1)}, s32[2,32]{1,0:T(2,128)S(1)}, u32[]{:S(2)}, u32[]{:S(2)}) collective-permute-start(s32[2,32]{1,0:T(2,128)S(1)} %shard_map.93.refs_0_), channel_id=1, source_target_pairs={{0,1},{1,2},{2,3},{3,0},{4,5},{5,6},{6,7},{7,4},{8,9},{9,10},{10,1... | collective-permute-start | bytes 776 | tf_op jit(solution)/shard_map/ppermute | solution.py:281
  20.8 3.9 %collective-permute-start.3 = (s32[2,32]{1,0:T(2,128)S(1)}, s32[2,32]{1,0:T(2,128)S(1)}, u32[]{:S(2)}, u32[]{:S(2)}) collective-permute-start(s32[2,32]{1,0:T(2,128)S(1)} %shard_map.93.refs_0_), channel_id=1, source_target_pairs={{0,2},{1,3},{2,0},{3,1},{4,6},{5,7},{6,4},{7,5},{8,10},{9,11},{10,... | collective-permute-start | bytes 776 | tf_op jit(solution)/shard_map/ppermute | solution.py:281
  23.2 2.4 %collective-permute-start.4 = (s32[2,32]{1,0:T(2,128)S(1)}, s32[2,32]{1,0:T(2,128)S(1)}, u32[]{:S(2)}, u32[]{:S(2)}) collective-permute-start(s32[2,32]{1,0:T(2,128)S(1)} %shard_map.93.refs_0_), channel_id=1, source_target_pairs={{0,3},{1,0},{2,1},{3,2},{4,7},{5,4},{6,5},{7,6},{8,11},{9,8},{10,9... | collective-permute-start | bytes 776 | tf_op jit(solution)/shard_map/ppermute | solution.py:281
  25.7 5.2 %collective-permute-start.5 = (s32[2,32]{1,0:T(2,128)S(1)}, s32[2,32]{1,0:T(2,128)S(1)}, u32[]{:S(2)}, u32[]{:S(2)}) collective-permute-start(s32[2,32]{1,0:T(2,128)S(1)} %shard_map.95.refs_0_), channel_id=1, source_target_pairs={{0,4},{1,5},{2,6},{3,7},{4,8},{5,9},{6,10},{7,11},{8,12},{9,13},{1... | collective-permute-start | bytes 776 | tf_op jit(solution)/shard_map/ppermute | solution.py:281
  27.2 3.9 %collective-permute-start.6 = (s32[2,32]{1,0:T(2,128)S(1)}, s32[2,32]{1,0:T(2,128)S(1)}, u32[]{:S(2)}, u32[]{:S(2)}) collective-permute-start(s32[2,32]{1,0:T(2,128)S(1)} %shard_map.95.refs_0_), channel_id=1, source_target_pairs={{0,8},{1,9},{2,10},{3,11},{4,12},{5,13},{6,14},{7,15},{8,0},{9,1},... | collective-permute-start | bytes 776 | tf_op jit(solution)/shard_map/ppermute | solution.py:281
  29.8 2.4 %collective-permute-start.7 = (s32[2,32]{1,0:T(2,128)S(1)}, s32[2,32]{1,0:T(2,128)S(1)}, u32[]{:S(2)}, u32[]{:S(2)}) collective-permute-start(s32[2,32]{1,0:T(2,128)S(1)} %shard_map.95.refs_0_), channel_id=1, source_target_pairs={{0,12},{1,13},{2,14},{3,15},{4,0},{5,1},{6,2},{7,3},{8,4},{9,5},{1... | collective-permute-start | bytes 776 | tf_op jit(solution)/shard_map/ppermute | solution.py:281
  32.3 3.5 %collective-permute-start.10 = (bf16[128,1280]{1,0:T(8,128)(2,1)S(1)}, bf16[128,1280]{1,0:T(8,128)(2,1)S(1)}, u32[]{:S(2)}, u32[]{:S(2)}) collective-permute-start(bf16[128,1280]{1,0:T(8,128)(2,1)S(1)} %shard_map.97), channel_id=1, source_target_pairs={{0,32},{1,33},{2,34},{3,35},{4,36},{5,37},{6,38},{7,39},{8,40},{9,... | collective-permute-start | bytes 983048 | tf_op jit(solution)/shard_map/ppermute | solution.py:255
  33.6 17.2 %collective-permute-start.16 = (bf16[128,1280]{1,0:T(8,128)(2,1)S(1)}, bf16[128,1280]{1,0:T(8,128)(2,1)S(1)}, u32[]{:S(2)}, u32[]{:S(2)}) collective-permute-start(bf16[128,1280]{1,0:T(8,128)(2,1)S(1)} %shard_map.97), channel_id=1, source_target_pairs={{0,96},{1,97},{2,98},{3,99},{4,100},{5,101},{6,102},{7,103},{8,104... | collective-permute-start | bytes 983048 | tf_op jit(solution)/shard_map/ppermute | solution.py:255
  38.3 7.0 %collective-permute-start.13 = (bf16[128,1280]{1,0:T(8,128)(2,1)S(1)}, bf16[128,1280]{1,0:T(8,128)(2,1)S(1)}, u32[]{:S(2)}, u32[]{:S(2)}) collective-permute-start(bf16[128,1280]{1,0:T(8,128)(2,1)S(1)} %shard_map.98.refs_7_), channel_id=1, source_target_pairs={{32,64},{33,65},{34,66},{35,67},{36,68},{37,69},{38,70},{39,71},{4... | collective-permute-start | bytes 983048 | tf_op jit(solution)/shard_map/ppermute | solution.py:255
  39.6 2.0 %collective-permute-start.11 = (bf16[128,1280]{1,0:T(8,128)(2,1)S(1)}, bf16[128,1280]{1,0:T(8,128)(2,1)S(1)}, u32[]{:S(2)}, u32[]{:S(2)}) collective-permute-start(bf16[128,1280]{1,0:T(8,128)(2,1)S(1)} %shard_map.99.refs_4_), channel_id=1, source_target_pairs={{0,32},{1,33},{2,34},{3,35},{4,36},{5,37},{6,38},{7,39},{8,40},{9,... | collective-permute-start | bytes 983048 | tf_op jit(solution)/shard_map/ppermute | solution.py:255
  39.7 11.2 %collective-permute-start.18 = (bf16[128,1280]{1,0:T(8,128)(2,1)S(1)}, bf16[128,1280]{1,0:T(8,128)(2,1)S(1)}, u32[]{:S(2)}, u32[]{:S(2)}) collective-permute-start(bf16[128,1280]{1,0:T(8,128)(2,1)S(1)} %shard_map.99.refs_4_), channel_id=1, source_target_pairs={{0,96},{1,97},{2,98},{3,99},{4,100},{5,101},{6,102},{7,103},{8,104... | collective-permute-start | bytes 983048 | tf_op jit(solution)/shard_map/ppermute | solution.py:255
  40.4 4.7 %collective-permute-start.14 = (bf16[256,1280]{1,0:T(8,128)(2,1)S(1)}, bf16[256,1280]{1,0:T(8,128)(2,1)S(1)}, u32[]{:S(2)}, u32[]{:S(2)}) collective-permute-start(bf16[256,1280]{1,0:T(8,128)(2,1)S(1)} %shard_map.100.refs_4_), channel_id=1, source_target_pairs={{0,32},{1,33},{2,34},{3,35},{4,36},{5,37},{6,38},{7,39},{8,40},{9,... | collective-permute-start | bytes 1966088 | tf_op jit(solution)/shard_map/ppermute | solution.py:255
  43.8 6.9 %collective-permute-start.12 = (bf16[128,1280]{1,0:T(8,128)(2,1)S(1)}, bf16[128,1280]{1,0:T(8,128)(2,1)S(1)}, u32[]{:S(2)}, u32[]{:S(2)}) collective-permute-start(bf16[128,1280]{1,0:T(8,128)(2,1)S(1)} %shard_map.101.refs_7_), channel_id=1, source_target_pairs={{32,64},{33,65},{34,66},{35,67},{36,68},{37,69},{38,70},{39,71},{4... | collective-permute-start | bytes 983048 | tf_op jit(solution)/shard_map/ppermute | solution.py:255
  45.2 5.5 %collective-permute-start.15 = (bf16[128,1280]{1,0:T(8,128)(2,1)S(1)}, bf16[128,1280]{1,0:T(8,128)(2,1)S(1)}, u32[]{:S(2)}, u32[]{:S(2)}) collective-permute-start(bf16[128,1280]{1,0:T(8,128)(2,1)S(1)} %shard_map.103.refs_4_), channel_id=1, source_target_pairs={{0,32},{1,33},{2,34},{3,35},{4,36},{5,37},{6,38},{7,39},{8,40},{9,... | collective-permute-start | bytes 983048 | tf_op jit(solution)/shard_map/ppermute | solution.py:255
  50.7 1.7 %collective-permute-start.17 = (bf16[128,1280]{1,0:T(8,128)(2,1)S(1)}, bf16[128,1280]{1,0:T(8,128)(2,1)S(1)}, u32[]{:S(2)}, u32[]{:S(2)}) collective-permute-start(bf16[128,1280]{1,0:T(8,128)(2,1)S(1)} %shard_map.104), channel_id=1, source_target_pairs={{0,32},{1,33},{2,34},{3,35},{4,36},{5,37},{6,38},{7,39},{8,40},{9,... | collective-permute-start | bytes 983048 | tf_op jit(solution)/shard_map/ppermute | solution.py:255
  52.4 2.6 %collective-permute-start.19 = (bf16[6,8,256]{2,1,0:T(8,128)(2,1)S(1)}, bf16[6,8,256]{2,1,0:T(8,128)(2,1)S(1)}, u32[]{:S(2)}, u32[]{:S(2)}) collective-permute-start(bf16[6,8,256]{2,1,0:T(8,128)(2,1)S(1)} %get-tuple-element.41), channel_id=1, source_target_pairs={{96,0},{97,1},{98,2},{99,3},{100,4},{101,5},{102,6},{103,7},{104,8... | collective-permute-start | bytes 73736 | tf_op jit(solution)/shard_map/ppermute | solution.py:255
  53.1 12.7 %collective-permute-start.20 = (bf16[6,8,256]{2,1,0:T(8,128)(2,1)S(1)}, bf16[6,8,256]{2,1,0:T(8,128)(2,1)S(1)}, u32[]{:S(2)}, u32[]{:S(2)}) collective-permute-start(bf16[6,8,256]{2,1,0:T(8,128)(2,1)S(1)} %get-tuple-element.42), channel_id=1, source_target_pairs={{96,32},{97,33},{98,34},{99,35},{100,36},{101,37},{102,38},{103,39... | collective-permute-start | bytes 73736 | tf_op jit(solution)/shard_map/ppermute | solution.py:255
  54.4 11.4 %collective-permute-start.21 = (bf16[6,8,256]{2,1,0:T(8,128)(2,1)S(1)}, bf16[6,8,256]{2,1,0:T(8,128)(2,1)S(1)}, u32[]{:S(2)}, u32[]{:S(2)}) collective-permute-start(bf16[6,8,256]{2,1,0:T(8,128)(2,1)S(1)} %get-tuple-element.43), channel_id=1, source_target_pairs={{96,64},{97,65},{98,66},{99,67},{100,68},{101,69},{102,70},{103,71... | collective-permute-start | bytes 73736 | tf_op jit(solution)/shard_map/ppermute | solution.py:255
